TPU v7x, 512 devices: a whole 4x8x8 slice. The times are simulated.
512 devices in a mesh: seg: 128 (over y_hi, z, x), tp: 4 (over y_lo, core).
Axes of the slice: x: 4, y: 8 (y_hi: 4, y_lo: 2; y = y_hi * 2 + y_lo), z: 8, core: 2. Of those that a mesh axis runs over, the one named last changes fastest.
Arguments:
- inputs: bfloat16 [16384, 2048], P('seg', 'tp'), may hold values from -40 to 40
- cotangent: bfloat16 [16384, 2048], P('seg', 'tp'), may hold values from -6 to 6
- w_query: bfloat16 [2, 2048, 2048], P(None, 'seg', 'tp'), may hold values from -1 to 1
- w_key: bfloat16 [2, 2048, 2048], P(None, 'seg', 'tp'), may hold values from -1 to 1
- w_value: bfloat16 [2, 2048, 2048], P(None, 'seg', 'tp'), may hold values from -0.25 to 0.25
- boundary: int32 [128], replicated, may hold values from 0 to 128, as said below
Outputs:
- outputs: bfloat16 [16384, 2048], P('seg', 'tp')
- input_grad: float32 [16384, 2048], P('seg', 'tp')
Inputs may be any that keep to these rules, and one draw needn't show every extreme that they name: `boundary`: the first segment's value is 0, the second's and the last segment's are 128; the value 128 means that no utterance begins in the segment.
All inputs are finite; a program needn't handle non-finite values.
Results may differ from a plain program's by a relative error of at most 0.035.
Values may be sent and summed in bfloat16 or wider, within the bound.
A program may use at most 64 MiB of HBM per device.

v0:
```python
import math

import jax
import jax.numpy as jnp
from jax import lax
from jax.sharding import PartitionSpec as P

HEAD = 128
LAYERS = 2


def passed_along(value, axis, steps):
    count = lax.axis_size(axis)
    first, last = (max(0, -steps), min(count, count - steps))
    return lax.ppermute(value, axis, [(source, source + steps) for source in range(first, last)])


def live_mask(boundary, row_count):
    seg_index = lax.axis_index("seg")
    bound_now = lax.dynamic_slice_in_dim(boundary, seg_index, 1)[0]
    bound_prev = lax.dynamic_slice_in_dim(boundary, jnp.maximum(seg_index - 1, 0), 1)[0]
    first_live = jnp.where(bound_prev == row_count, 0, bound_prev)
    positions = jnp.arange(row_count, dtype=jnp.int32)
    query_pos = positions[:, None]
    key_pos = positions[None, :]
    from_memory = (query_pos < bound_now) & (key_pos >= first_live) & (seg_index > 0)
    from_segment = (key_pos <= query_pos) & jnp.logical_not(
        (key_pos < bound_now) & (query_pos >= bound_now)
    )
    return jnp.concatenate([from_memory, from_segment], axis=1)[None]


def project(gathered, weight):
    return jnp.dot(gathered, weight, preferred_element_type=jnp.float32).astype(jnp.bfloat16)


def fetch_layer(w_query, w_key, w_value, layer_id):
    return (
        lax.all_gather(w_query[layer_id], "seg", axis=0, tiled=True),
        lax.all_gather(w_key[layer_id], "seg", axis=0, tiled=True),
        lax.all_gather(w_value[layer_id], "seg", axis=0, tiled=True),
    )


def forward_layer(states, weights, visible):
    query_weight, key_weight, value_weight = weights
    row_count = states.shape[0]
    local_width = query_weight.shape[1]
    local_heads = local_width // HEAD
    score_scale = 1.0 / math.sqrt(HEAD)
    gathered = lax.all_gather(states, "tp", axis=1, tiled=True)
    queries = project(gathered, query_weight)
    key_rows = project(gathered, key_weight)
    value_rows = project(gathered, value_weight)
    memory_keys, memory_values = passed_along((key_rows, value_rows), "seg", 1)
    all_keys = jnp.concatenate([memory_keys, key_rows], axis=0).reshape(
        2 * row_count, local_heads, HEAD
    )
    all_values = jnp.concatenate([memory_values, value_rows], axis=0).reshape(
        2 * row_count, local_heads, HEAD
    )
    query_heads = queries.reshape(row_count, local_heads, HEAD)
    scores = (
        jnp.einsum("rhe,jhe->hrj", query_heads, all_keys, preferred_element_type=jnp.float32)
        * score_scale
    )
    scores = jnp.where(visible, scores, -1e30)
    maxima = jnp.max(scores, axis=-1, keepdims=True)
    raised = jnp.exp(scores - maxima)
    attn_weights = (raised / jnp.sum(raised, axis=-1, keepdims=True)).astype(jnp.bfloat16)
    attended = jnp.einsum(
        "hrj,jhe->rhe", attn_weights, all_values, preferred_element_type=jnp.float32
    )
    following = (states.astype(jnp.float32) + attended.reshape(row_count, local_width)).astype(
        jnp.bfloat16
    )
    return (following, (query_heads, all_keys, all_values, attn_weights))


def backward_layer(grad, saved, weights):
    query_weight, key_weight, value_weight = weights
    query_heads, all_keys, all_values, attn_weights = saved
    row_count = grad.shape[0]
    local_width = query_weight.shape[1]
    local_heads = local_width // HEAD
    score_scale = 1.0 / math.sqrt(HEAD)
    grad_out = grad.astype(jnp.bfloat16).reshape(row_count, local_heads, HEAD)
    grad_probs = jnp.einsum(
        "rhe,jhe->hrj", grad_out, all_values, preferred_element_type=jnp.float32
    )
    weights_float = attn_weights.astype(jnp.float32)
    row_dots = jnp.sum(weights_float * grad_probs, axis=-1, keepdims=True)
    grad_scores = (weights_float * (grad_probs - row_dots) * score_scale).astype(jnp.bfloat16)
    grad_query = jnp.einsum(
        "hrj,jhe->rhe", grad_scores, all_keys, preferred_element_type=jnp.float32
    )
    grad_keys = jnp.einsum(
        "hrj,rhe->jhe", grad_scores, query_heads, preferred_element_type=jnp.float32
    )
    grad_values = jnp.einsum(
        "hrj,rhe->jhe", attn_weights, grad_out, preferred_element_type=jnp.float32
    )
    grad_keys = grad_keys.reshape(2 * row_count, local_width)
    grad_values = grad_values.reshape(2 * row_count, local_width)
    later_keys, later_values = passed_along(
        (grad_keys[:row_count], grad_values[:row_count]), "seg", -1
    )
    key_part = (grad_keys[row_count:] + later_keys).astype(jnp.bfloat16)
    value_part = (grad_values[row_count:] + later_values).astype(jnp.bfloat16)
    query_part = grad_query.reshape(row_count, local_width).astype(jnp.bfloat16)
    partial_value = jnp.dot(query_part, query_weight.T, preferred_element_type=jnp.float32)
    partial_value = partial_value + jnp.dot(
        key_part, key_weight.T, preferred_element_type=jnp.float32
    )
    partial_value = partial_value + jnp.dot(
        value_part, value_weight.T, preferred_element_type=jnp.float32
    )
    return grad + lax.psum_scatter(partial_value, "tp", scatter_dimension=1, tiled=True)


def per_device(inputs, cotangent, w_query, w_key, w_value, boundary):
    row_count = inputs.shape[0]
    visible = live_mask(boundary, row_count)
    layer_sets = [fetch_layer(w_query, w_key, w_value, layer_id) for layer_id in range(LAYERS)]
    states = inputs
    saved_all = []
    for layer_id in range(LAYERS):
        states, saved = forward_layer(states, layer_sets[layer_id], visible)
        saved_all.append(saved)
    grad = cotangent.astype(jnp.float32)
    for layer_id in reversed(range(LAYERS)):
        grad = backward_layer(grad, saved_all[layer_id], layer_sets[layer_id])
    return (states, grad)


def solution(mesh):
    return jax.shard_map(
        per_device,
        mesh=mesh,
        in_specs=(
            P("seg", "tp"),
            P("seg", "tp"),
            P(None, "seg", "tp"),
            P(None, "seg", "tp"),
            P(None, "seg", "tp"),
            P(),
        ),
        out_specs=(P("seg", "tp"), P("seg", "tp")),
        check_vma=False,
    )
```

profile of v0, /device:TPU:6, one launch (start us, length us, event | category | flops | bytes accessed | tf_op | source)
XLA Modules:
  0.0 905.1 jit_solution(1071539472231299652)
XLA Ops:
  7.2 1.3 fusion.113
  8.6 1.3 fusion.112
  10.1 1.4 fusion.114
  11.5 0.5 all-gather.23.cloned.1.call-update
  12.1 0.5 all-gather.19.cloned.1.call-update
  12.6 0.5 all-gather.21.cloned.1.call-update
  13.2 1.3 fusion.115
  15.8 1.0 copy.32
  16.9 0.6 iota_compare_fusion.1
  17.6 7.5 all_gather.24
  25.1 116.1 %all-gather.17.cloned.1.call-done = bf16[1,2048,512]{2,1,0:T(8,128)(2,1)} async-done(((bf16[1,16,512]{2,1,0:T(8,128)(2,1)}), bf16[1,2048,512]{2,1,0:T(8,128)(2,1)}) %all-gather.17.cloned.1.call-update) | async-done | bytes 2097168 | tf_op jit(solution)/shard_map/all_gather | solution.py:40
  141.2 2.0 fusion.44
  143.2 2.6 collective-permute-start.1
  145.8 119.8 %all-gather.13.cloned.1.call-done = bf16[1,2048,512]{2,1,0:T(8,128)(2,1)} async-done(((bf16[1,16,512]{2,1,0:T(8,128)(2,1)}), bf16[1,2048,512]{2,1,0:T(8,128)(2,1)}) %all-gather.13.cloned.1.call-update) | async-done | bytes 2097168 | tf_op jit(solution)/shard_map/all_gather | solution.py:41
  265.6 2.0 fusion.38
  267.6 122.9 %all-gather.15.cloned.1.call-done = bf16[1,2048,512]{2,1,0:T(8,128)(2,1)} async-done(((bf16[1,16,512]{2,1,0:T(8,128)(2,1)}), bf16[1,2048,512]{2,1,0:T(8,128)(2,1)}) %all-gather.15.cloned.1.call-update) | async-done | bytes 2097168 | tf_op jit(solution)/shard_map/all_gather | solution.py:39
  390.6 2.0 fusion.41
  392.8 2.7 collective-permute-start
  395.7 0.4 fusion.116
  396.3 3.5 collective-permute-done
  399.8 0.3 fusion.75
  400.2 6.5 all_gather.28
  406.7 108.1 %all-gather.23.cloned.1.call-done = bf16[1,2048,512]{2,1,0:T(8,128)(2,1)} async-done(((bf16[1,16,512]{2,1,0:T(8,128)(2,1)}), bf16[1,2048,512]{2,1,0:T(8,128)(2,1)}) %all-gather.23.cloned.1.call-update) | async-done | bytes 2097168 | tf_op jit(solution)/shard_map/all_gather | solution.py:40
  514.8 2.0 fusion.53
  516.9 2.6 collective-permute-start.3
  519.5 119.6 %all-gather.19.cloned.1.call-done = bf16[1,2048,512]{2,1,0:T(8,128)(2,1)} async-done(((bf16[1,16,512]{2,1,0:T(8,128)(2,1)}), bf16[1,2048,512]{2,1,0:T(8,128)(2,1)}) %all-gather.19.cloned.1.call-update) | async-done | bytes 2097168 | tf_op jit(solution)/shard_map/all_gather | solution.py:41
  639.1 2.0 fusion.47
  641.1 122.2 %all-gather.21.cloned.1.call-done = bf16[1,2048,512]{2,1,0:T(8,128)(2,1)} async-done(((bf16[1,16,512]{2,1,0:T(8,128)(2,1)}), bf16[1,2048,512]{2,1,0:T(8,128)(2,1)}) %all-gather.21.cloned.1.call-update) | async-done | bytes 2097168 | tf_op jit(solution)/shard_map/all_gather | solution.py:39
  763.3 2.0 fusion.50
  765.5 2.6 collective-permute-start.2
  768.3 0.4 fusion.117
  768.9 3.5 collective-permute-done.2
  772.4 0.6 copy-done.14
  773.0 0.3 convolution_bitcast_fusion.4
  773.3 0.8 copy-done.12
  774.1 2.1 convolution_convert_fusion.1
  776.2 1.6 convolution_bitcast_fusion.3
  777.7 0.2 convolution_bitcast_fusion
  778.0 2.8 collective-permute-start.5
  780.8 2.5 collective-permute-start.4
  783.3 0.8 fusion.7
  784.1 4.3 collective-permute-done.5
  788.5 2.8 collective-permute-done.4
  791.3 0.8 convolution_add_fusion.3
  792.1 0.7 copy-done.4
  792.9 1.8 convolution_add_fusion.2
  794.8 35.6 %reduce-scatter.3.cloned.1.call-done = f32[128,512]{1,0:T(8,128)} async-done(((f32[128,2048]{1,0:T(8,128)}), f32[128,512]{1,0:T(8,128)}) %reduce-scatter.3.cloned.1.call-update) | async-done | bytes 262160 | tf_op jit(solution)/shard_map/reduce_scatter | solution.py:118
  830.4 1.0 fusion.92
  831.5 1.1 fusion.77
  832.6 2.4 convolution_convert_fusion
  835.0 1.6 convolution_bitcast_fusion.2
  836.6 0.2 convolution_bitcast_fusion.1
  836.9 2.9 collective-permute-start.7
  839.8 2.4 collective-permute-start.6
  842.3 0.8 fusion.17
  843.1 6.9 collective-permute-done.7
  850.1 4.9 collective-permute-done.6
  855.0 0.8 convolution_add_fusion.1
  855.9 0.7 copy-done.1
  856.6 1.8 convolution_add_fusion
  858.5 0.3 fusion.72
  858.9 0.7 add_convert_fusion
  859.6 37.0 %reduce-scatter.5.cloned.1.call-done = f32[128,512]{1,0:T(8,128)} async-done(((f32[128,2048]{1,0:T(8,128)}), f32[128,512]{1,0:T(8,128)}) %reduce-scatter.5.cloned.1.call-update) | async-done | bytes 262160 | tf_op jit(solution)/shard_map/reduce_scatter | solution.py:118
  896.6 1.7 fusion.91
  (82 shorter events, 2.2 us)
Async XLA Ops:
  7.2 134.0 %all-gather.17.cloned.1.call-start = ((), (), s32[]{:S(2)}) async-start(), calls=%async_computation.6 | async-start | bytes 2113536 | tf_op jit(solution)/shard_map/all_gather | solution.py:40
  8.6 257.0 %all-gather.13.cloned.1.call-start = ((), (), s32[]{:S(2)}) async-start(), calls=%async_computation.4 | async-start | bytes 2113536 | tf_op jit(solution)/shard_map/all_gather | solution.py:41
  10.0 380.6 %all-gather.15.cloned.1.call-start = ((), (), s32[]{:S(2)}) async-start(), calls=%async_computation.5 | async-start | bytes 2113536 | tf_op jit(solution)/shard_map/all_gather | solution.py:39
  11.4 503.4 %all-gather.23.cloned.1.call-start = ((), (), s32[]{:S(2)}) async-start(), calls=%async_computation.9 | async-start | bytes 2113536 | tf_op jit(solution)/shard_map/all_gather | solution.py:40
  12.0 627.1 %all-gather.19.cloned.1.call-start = ((), (), s32[]{:S(2)}) async-start(), calls=%async_computation.7 | async-start | bytes 2113536 | tf_op jit(solution)/shard_map/all_gather | solution.py:41
  12.6 750.7 %all-gather.21.cloned.1.call-start = ((), (), s32[]{:S(2)}) async-start(), calls=%async_computation.8 | async-start | bytes 2113536 | tf_op jit(solution)/shard_map/all_gather | solution.py:39
  13.2 817.2 %reduce-scatter.3.cloned.1.call-start = ((), (), s32[]{:S(2)}) async-start(), calls=%async_computation.2 | async-start | bytes 1310720 | tf_op jit(solution)/shard_map/reduce_scatter | solution.py:118
  143.2 252.2 %collective-permute-start.1 = (bf16[128,512]{1,0:T(8,128)(2,1)S(1)}, bf16[128,512]{1,0:T(8,128)(2,1)S(1)}, u32[]{:S(2)}, u32[]{:S(2)}) collective-permute-start(bf16[128,512]{1,0:T(8,128)(2,1)S(1)} %fusion.44), channel_id=1, source_target_pairs={{0,4},{4,8},{8,12},{12,16},{16,20},{20,24},{24,28},{28,32},{32,36}... | collective-permute-start | bytes 393224 | tf_op jit(solution)/shard_map/ppermute | solution.py:15
  267.6 132.1 %copy-start.9 = (bf16[128,512]{1,0:T(8,128)(2,1)}, bf16[128,512]{1,0:T(8,128)(2,1)S(1)}, u32[]{:S(2)}) copy-start(bf16[128,512]{1,0:T(8,128)(2,1)S(1)} %fusion.38) | copy-start | bytes 393220
  392.7 7.4 copy-start.18
  392.7 7.4 copy-start.13
  392.8 7.0 collective-permute-start
  395.7 11.1 %copy-start.20 = (bf16[256,512]{0,1:T(8,128)(2,1)}, bf16[256,512]{0,1:T(8,128)(2,1)S(1)}, u32[]{:S(2)}) copy-start(bf16[256,512]{0,1:T(8,128)(2,1)S(1)} %copy.29) | copy-start | bytes 786436
  399.8 117.1 %copy-start.16 = (bf16[128,512]{1,0:T(8,128)(2,1)}, bf16[128,512]{1,0:T(8,128)(2,1)S(1)}, u32[]{:S(2)}) copy-start(bf16[128,512]{1,0:T(8,128)(2,1)S(1)} %collective-permute-done) | copy-start | bytes 393220
  516.9 251.2 %collective-permute-start.3 = (bf16[128,512]{1,0:T(8,128)(2,1)S(1)}, bf16[128,512]{1,0:T(8,128)(2,1)S(1)}, u32[]{:S(2)}, u32[]{:S(2)}) collective-permute-start(bf16[128,512]{1,0:T(8,128)(2,1)S(1)} %fusion.53), channel_id=1, source_target_pairs={{0,4},{4,8},{8,12},{12,16},{16,20},{20,24},{24,28},{28,32},{32,36}... | collective-permute-start | bytes 393224 | tf_op jit(solution)/shard_map/ppermute | solution.py:15
  641.1 131.3 %copy-start.7 = (bf16[128,512]{1,0:T(8,128)(2,1)}, bf16[128,512]{1,0:T(8,128)(2,1)S(1)}, u32[]{:S(2)}) copy-start(bf16[128,512]{1,0:T(8,128)(2,1)S(1)} %fusion.47) | copy-start | bytes 393220
  765.5 6.9 copy-start.19
  765.5 6.9 collective-permute-start.2
  768.3 4.1 copy-start.21
  772.4 0.7 copy-start.14
  773.3 0.8 copy-start.12
  774.1 9.2 %copy-start.5 = (bf16[1,2048,512]{2,1,0:T(8,128)(2,1)S(1)}, bf16[1,2048,512]{2,1,0:T(8,128)(2,1)}, u32[]{:S(2)}) copy-start(bf16[1,2048,512]{2,1,0:T(8,128)(2,1)} %all-gather.21.cloned.1.call-done) | copy-start | bytes 6291460
  777.7 5.6 copy-start.23
  778.0 10.4 %collective-permute-start.5 = (f32[128,512]{0,1:T(8,128)S(1)}, f32[128,512]{0,1:T(8,128)S(1)}, u32[]{:S(2)}, u32[]{:S(2)}) collective-permute-start(f32[128,512]{0,1:T(8,128)S(1)} %bitcast.158), channel_id=1, source_target_pairs={{4,0},{8,4},{12,8},{16,12},{20,16},{24,20},{28,24},{32,28},{36,32}... | collective-permute-start | bytes 786440 | tf_op jit(solution)/shard_map/ppermute | solution.py:15
  780.8 10.4 %collective-permute-start.4 = (f32[128,512]{0,1:T(8,128)S(1)}, f32[128,512]{0,1:T(8,128)S(1)}, u32[]{:S(2)}, u32[]{:S(2)}) collective-permute-start(f32[128,512]{0,1:T(8,128)S(1)} %bitcast.156), channel_id=1, source_target_pairs={{4,0},{8,4},{12,8},{16,12},{20,16},{24,20},{28,24},{32,28},{36,32}... | collective-permute-start | bytes 786440 | tf_op jit(solution)/shard_map/ppermute | solution.py:15
  783.3 8.0 copy-start.3
  791.3 1.6 copy-start.4
  792.9 37.5 %copy-start.6 = (bf16[128,512]{1,0:T(8,128)(2,1)S(1)}, bf16[128,512]{1,0:T(8,128)(2,1)}, u32[]{:S(2)}) copy-start(bf16[128,512]{1,0:T(8,128)(2,1)} %param.7) | copy-start | bytes 393220
  792.9 38.6 %copy-start.10 = (bf16[128,512]{1,0:T(8,128)(2,1)S(1)}, bf16[128,512]{1,0:T(8,128)(2,1)}, u32[]{:S(2)}) copy-start(bf16[128,512]{1,0:T(8,128)(2,1)} %copy-done.9) | copy-start | bytes 393220
  792.9 38.6 %copy-start.17 = (bf16[128,512]{1,0:T(8,128)(2,1)S(1)}, bf16[128,512]{1,0:T(8,128)(2,1)}, u32[]{:S(2)}) copy-start(bf16[128,512]{1,0:T(8,128)(2,1)} %copy-done.16) | copy-start | bytes 393220
  794.7 101.9 %reduce-scatter.5.cloned.1.call-start = ((), (), s32[]{:S(2)}) async-start(), calls=%async_computation.3 | async-start | bytes 1310720 | tf_op jit(solution)/shard_map/reduce_scatter | solution.py:118
  832.6 9.7 %copy-start.2 = (bf16[1,2048,512]{2,1,0:T(8,128)(2,1)S(1)}, bf16[1,2048,512]{2,1,0:T(8,128)(2,1)}, u32[]{:S(2)}) copy-start(bf16[1,2048,512]{2,1,0:T(8,128)(2,1)} %all-gather.15.cloned.1.call-done) | copy-start | bytes 6291460
  836.6 5.7 copy-start.22
  836.9 13.1 %collective-permute-start.7 = (f32[128,512]{0,1:T(8,128)S(1)}, f32[128,512]{0,1:T(8,128)S(1)}, u32[]{:S(2)}, u32[]{:S(2)}) collective-permute-start(f32[128,512]{0,1:T(8,128)S(1)} %bitcast.159), channel_id=1, source_target_pairs={{4,0},{8,4},{12,8},{16,12},{20,16},{24,20},{28,24},{32,28},{36,32}... | collective-permute-start | bytes 786440 | tf_op jit(solution)/shard_map/ppermute | solution.py:15
  839.8 15.2 %collective-permute-start.6 = (f32[128,512]{0,1:T(8,128)S(1)}, f32[128,512]{0,1:T(8,128)S(1)}, u32[]{:S(2)}, u32[]{:S(2)}) collective-permute-start(f32[128,512]{0,1:T(8,128)S(1)} %bitcast.157), channel_id=1, source_target_pairs={{4,0},{8,4},{12,8},{16,12},{20,16},{24,20},{28,24},{32,28},{36,32}... | collective-permute-start | bytes 786440 | tf_op jit(solution)/shard_map/ppermute | solution.py:15
  842.3 12.7 %copy-start = (bf16[1,2048,512]{2,1,0:T(8,128)(2,1)S(1)}, bf16[1,2048,512]{2,1,0:T(8,128)(2,1)}, u32[]{:S(2)}) copy-start(bf16[1,2048,512]{2,1,0:T(8,128)(2,1)} %all-gather.17.cloned.1.call-done) | copy-start | bytes 6291460
  855.0 1.6 copy-start.1
  856.6 1.8 copy-start.8
  856.6 1.9 copy-start.15
  858.4 38.2 %copy-start.11 = (f32[128,512]{1,0:T(8,128)S(1)}, f32[128,512]{1,0:T(8,128)}, u32[]{:S(2)}) copy-start(f32[128,512]{1,0:T(8,128)} %reduce-scatter.3.cloned.1.call-done) | copy-start | bytes 786436
Sparse Core Ops, SparseCore 0:
  13.1 128.0 all-gather.16
  145.7 119.8 all-gather.12
  270.6 119.8 all-gather.14
  394.9 119.8 all-gather.22
  519.1 119.8 all-gather.18
  643.4 119.8 all-gather.20
  794.8 35.5 reduce-scatter.2
  858.6 37.9 reduce-scatter.4
where the time goes:
time: 907 us; the launch traced here: 905 us
  waiting for transfers between devices  809 us (89%)
  matrix products  29.9 us (3%)
  starting transfers between devices  21.3 us (2%)
  between operations  16 us (2%)
  blocking collectives  14 us (2%)
  local copies, waits for them, and re-layouts  10.5 us (1%)
    all_gather x2, waiting for transfers between devices, fetch_layer(): lax.all_gather(w_query[layer_id], 'seg', axis=0, tiled=True)  245 us
    all_gather x2, waiting for transfers between devices, fetch_layer(): lax.all_gather(w_value[layer_id], 'seg', axis=0, tiled=True)  239 us
    all_gather x2, waiting for transfers between devices, fetch_layer(): lax.all_gather(w_key[layer_id], 'seg', axis=0, tiled=True)  224 us
    reduce_scatter x2, waiting for transfers between devices, backward_layer(): lax.psum_scatter(partial_value, 'tp', scatter_dimension=1, tiled=True)  72.6 us
    ppermute x8, waiting for transfers between devices, passed_along(): lax.ppermute(value, axis, [(source, source + steps) for source in range(f...  25.8 us
    ppermute x8, starting transfers between devices, passed_along(): lax.ppermute(value, axis, [(source, source + steps) for source in range(f...  21 us
  transfers between devices with their start and end apart: 16, of which 14 were waited for; matrix products, arithmetic and copies ran while one was open for 3% of the time, Pallas kernels for 0%

commit v1 on v0

v1 whole, which is shorter than its diff:
```python
import math

import jax
import jax.numpy as jnp
from jax import lax
from jax.experimental import pallas as pl
from jax.experimental.pallas import tpu as pltpu
from jax.sharding import PartitionSpec as P

MESH = pl.DeviceIdType.MESH
HEAD = 128
LAYERS = 2
ROWS = 128
D = 2048
GROUP_ROWS = 2 * ROWS
BLK = 2 * HEAD
SCALE = 1.0 / math.sqrt(HEAD)
N_SEND = 176
N_RECV = 176
BF = jnp.bfloat16
F32 = jnp.float32


def nt(a, b):
    return lax.dot_general(a, b, (((1,), (1,)), ((), ())), preferred_element_type=F32)


def nn(a, b):
    return lax.dot_general(a, b, (((1,), (0,)), ((), ())), preferred_element_type=F32)


def tn(a, b):
    return lax.dot_general(a, b, (((0,), (0,)), ((), ())), preferred_element_type=F32)


def kernel(
    x_in, cot_in, wq, wk, wv, bound,
    out_ref, grad_ref,
    stage, w, x0, x1, cotg, kv, q, probs, dkv, halo_send, halo_recv, dqkv,
    swap_send, swap_recv, own, rs_send, rs1_recv, rs0_recv, x2, outbuf, g1,
    ssem, rsem,
):
    seg = lax.axis_index("seg")
    tp = lax.axis_index("tp")
    x = lax.rem(seg, 4)
    z = lax.rem(lax.div(seg, 4), 8)
    yh = lax.div(seg, 32)
    yl = lax.div(tp, 2)
    c = lax.rem(tp, 2)
    y = yh * 2 + yl
    other = 1 - c
    xh = lax.div(x, 2)
    xl = lax.rem(x, 2)

    def dev(dx, dy, dz, dc):
        return (lax.div(dy, 2) * 32 + dz * 4 + dx, lax.rem(dy, 2) * 2 + dc)

    def wrap(value, n):
        return lax.rem(value + n, n)

    me_y = y
    pair_y = yh * 2 + (1 - yl)
    group = yh * 16 + z * 2 + yl
    after = wrap(group + 1, 64)
    before = wrap(group - 1, 64)

    def group_dev(g):
        gy = lax.div(g, 16) * 2 + lax.rem(g, 2)
        return dev(x, gy, lax.rem(lax.div(g, 2), 8), c)

    partner = dev(x, y, z, other)
    peers = [dev(wrap(x + k, 4), y, z, c) for k in (1, 2, 3)]

    counts = {"s": 0, "r": 0}
    pending = []

    def take(kind, n=1):
        first = counts[kind]
        counts[kind] += n
        return first

    def send(src, dst, recv, target, cond=None):
        copy = pltpu.make_async_remote_copy(
            src_ref=src, dst_ref=dst, send_sem=ssem.at[take("s")], recv_sem=rsem.at[recv],
            device_id=target, device_id_type=MESH,
        )
        if cond is None:
            copy.start()
        else:
            pl.when(cond)(copy.start)
        pending.append((copy, cond))

    def arrive(dst, recv, cond=None):
        copy = pltpu.make_async_remote_copy(
            src_ref=dst, dst_ref=dst, send_sem=ssem.at[0], recv_sem=rsem.at[recv],
            device_id=partner, device_id_type=MESH,
        )
        if cond is None:
            copy.wait_recv()
        else:
            pl.when(cond)(copy.wait_recv)

    for layer in range(LAYERS):
        for j in range(2):
            for t, ref in enumerate((wq, wk, wv)):
                stage[j, layer, :, t * BLK:(t + 1) * BLK] = ref[layer, :, j * BLK:(j + 1) * BLK]

    barrier = pltpu.get_barrier_semaphore()
    known = list(peers) + [partner, group_dev(after), group_dev(before)]
    known += [dev(wrap(x + k, 4), pair_y, z, c) for k in (1, 2, 3)]
    known += [dev(x, y, wrap(z + k, 8), c) for k in range(1, 8)]
    known += [dev(x, wrap(y + k, 8), z, c) for k in range(1, 8)]
    for device in known:
        pl.semaphore_signal(barrier, inc=1, device_id=device, device_id_type=MESH)
    pl.semaphore_wait(barrier, len(known))

    same = xh == yl
    home = [same & (xl == j) for j in range(2)]
    away = [jnp.logical_not(h) for h in home]
    dest_y = yh * 2 + xh
    own_col = pl.multiple_of(xh * 1024 + c * 512 + xl * BLK, BLK)

    a2a_w = [take("r", 2) for _ in range(LAYERS)]
    a2a_c = take("r", 2)

    def spread_weights(layer):
        for j in range(2):
            dst = w.at[layer, yh, z, xh, xl]
            send(stage.at[j, layer], dst, a2a_w[layer] + xl, dev(2 * yl + j, dest_y, z, c), away[j])

            @pl.when(home[j])
            def _():
                w[layer, yh, z, xh, xl] = stage[j, layer]

    def spread_weights_wait(layer):
        for k in range(2):
            arrive(w.at[layer, yh, z, yl, k], a2a_w[layer] + k, away[k])

    spread_weights(0)
    spread_weights(1)

    x0_x = [[take("r") for _ in range(2)] for _ in range(2)]
    x0_c = [[take("r") for _ in range(2)] for _ in range(2)]
    my_rows = pl.multiple_of(xl * ROWS, ROWS)
    my_cols = pl.multiple_of(tp * 512, 512)

    @pl.when(same)
    def _():
        x0[pl.ds(my_rows, ROWS), pl.ds(my_cols, 512)] = x_in[...]

    send(
        x_in, x0.at[pl.ds(my_rows, ROWS), pl.ds(my_cols, 512)], x0_x[0][0] + xl * 2 + yl,
        dev(x, pair_y, z, c), jnp.logical_not(same),
    )

    def x0_piece(j, half, core):
        return x0.at[pl.ds(j * ROWS, ROWS), pl.ds(pl.multiple_of(half * 1024 + core * 512, 512), 512)]

    def x0_step(j, half, local):
        piece = x0_piece(j, half, c)
        here = home[j] & (yl == half)
        if not local:
            arrive(piece, x0_x[j][half], jnp.logical_not(here))
        for target in peers:
            cond = here if local else home[j] & (yl != half)
            send(piece, piece, x0_x[j][half], target, cond)

    def x0_swap(j, half):
        piece = x0_piece(j, half, c)
        send(piece, piece, x0_c[j][half], partner)

    for j in range(2):
        for half in range(2):
            x0_step(j, half, True)

    for j in range(2):
        dst = cotg.at[pl.ds(my_rows, ROWS)]
        src = cot_in.at[:, pl.ds(j * BLK, BLK)]
        send(src, dst, a2a_c + xl, dev(2 * yl + j, dest_y, z, c), away[j])

        @pl.when(home[j])
        def _():
            cotg[pl.ds(my_rows, ROWS)] = cot_in[:, j * BLK:(j + 1) * BLK]

    one = [[take("r", 7) for _ in range(2)] for _ in range(LAYERS)]
    two = {
        (layer, kind, right, s, d): take("r")
        for layer in range(LAYERS) for d in range(1, 5) for kind in range(2) for right in range(2) for s in range(2)
        if d <= (4 if right == s else 3)
    }

    def phase_one(layer):
        for k in range(1, 8):
            a = w.at[layer, yh, z, yl, 0]
            send(a, a, one[layer][0] + k - 1, dev(x, y, wrap(z + k, 8), c))
            b = w.at[layer, yh, z, yl, 1]
            send(b, b, one[layer][1] + k - 1, dev(x, wrap(y + k, 8), z, c))

    def phase_one_wait(layer):
        for k in range(1, 8):
            arrive(w.at[layer, yh, wrap(z - k, 8), yl, 0], one[layer][0] + k - 1)
            ys = wrap(y - k, 8)
            arrive(w.at[layer, lax.div(ys, 2), z, lax.rem(ys, 2), 1], one[layer][1] + k - 1)

    def chunk(layer, kind, right, s, d):
        if kind == 0:
            ys = wrap(y - d if right else y + d, 8)
            return w.at[layer, lax.div(ys, 2), pl.ds(4 * s, 4), lax.rem(ys, 2), 0]
        zs = wrap(z - d if right else z + d, 8)
        return w.at[layer, pl.ds(2 * s, 2), zs, :, 1]

    def forward(layer, kind, right, s, d):
        step = 1 if right else -1
        target = dev(x, wrap(y + step, 8), z, c) if kind == 0 else dev(x, y, wrap(z + step, 8), c)
        piece = chunk(layer, kind, right, s, d)
        send(piece, piece, two[layer, kind, right, s, d + 1], target)

    def phase_two(layer, d):
        for s in range(2):
            for kind in range(2):
                for right in range(2):
                    most = 4 if right == s else 3
                    if d > most:
                        continue
                    if d > 0:
                        arrive(chunk(layer, kind, right, s, d), two[layer, kind, right, s, d])
                    if d < most:
                        forward(layer, kind, right, s, d)

    spread_weights_wait(0)
    phase_one(0)
    spread_weights_wait(1)
    phase_one_wait(0)
    phase_two(0, 0)
    phase_one(1)
    for j in range(2):
        for half in range(2):
            x0_step(j, half, False)
    phase_two(0, 1)
    for j in range(2):
        for half in range(2):
            x0_swap(j, half)
    phase_two(0, 2)
    phase_two(0, 3)
    phase_one_wait(1)
    phase_two(1, 0)
    phase_two(0, 4)
    for j in range(2):
        for half in range(2):
            arrive(x0_piece(j, half, other), x0_c[j][half])

    pos_q = lax.broadcasted_iota(jnp.int32, (ROWS, GROUP_ROWS), 0)
    pos_k = lax.broadcasted_iota(jnp.int32, (ROWS, GROUP_ROWS), 1)

    def mask(j):
        s = 2 * group + j
        now = bound[s]
        prev = bound[jnp.maximum(s - 1, 0)]
        first = jnp.where(prev == ROWS, 0, prev)
        first = jnp.where(s > 0, first, ROWS)
        pos_m = pos_k - ROWS
        memory = (pos_k < ROWS) & (pos_q < now) & (pos_k >= first)
        segment = (pos_m >= 0) & (pos_m <= pos_q) & ((pos_m >= now) | (pos_q < now))
        return memory | segment

    halo_f = [take("r") for _ in range(LAYERS)]
    halo_b = [take("r") for _ in range(LAYERS)]

    def project(layer, states):
        total = None
        for part in range(4):
            weight = w[layer, part].reshape(512, 3 * BLK)
            term = nn(states[:, part * 512:(part + 1) * 512], weight)
            total = term if total is None else total + term
        total = total.astype(BF)
        q[layer] = total[:, :BLK]
        kv[layer, ROWS:, :] = total[:, BLK:]
        tail = kv.at[layer, pl.ds(2 * ROWS, ROWS)]
        send(tail, kv.at[layer, pl.ds(0, ROWS)], halo_f[layer], group_dev(after))

    def attend(layer, j):
        visible = mask(j)
        results = []
        for h in range(2):
            cols = slice(h * HEAD, (h + 1) * HEAD)
            vcols = slice(BLK + h * HEAD, BLK + (h + 1) * HEAD)
            queries = q[layer, j * ROWS:(j + 1) * ROWS, cols]
            keys = kv[layer, j * ROWS:(j + 2) * ROWS, cols]
            values = kv[layer, j * ROWS:(j + 2) * ROWS, vcols]
            scores = jnp.where(visible, nt(queries, keys) * SCALE, -1e30)
            raised = jnp.exp(scores - jnp.max(scores, axis=-1, keepdims=True))
            share = (raised / jnp.sum(raised, axis=-1, keepdims=True)).astype(BF)
            probs[layer, j, h] = share
            results.append(nn(share, values))
        return jnp.concatenate(results, axis=1)

    def x1_piece(j, xs, core):
        col = lax.div(xs, 2) * 1024 + core * 512 + lax.rem(xs, 2) * BLK
        return x1.at[pl.ds(j * ROWS, ROWS), pl.ds(pl.multiple_of(col, BLK), BLK)]

    x1_x = [take("r", 3) for _ in range(2)]
    x1_c = [take("r", 4) for _ in range(2)]

    def step_states(j):
        before_states = x0[j * ROWS:(j + 1) * ROWS, pl.ds(own_col, BLK)]
        x1[j * ROWS:(j + 1) * ROWS, pl.ds(own_col, BLK)] = (
            before_states.astype(F32) + attend(0, j)
        ).astype(BF)
        piece = x1_piece(j, x, c)
        for k in range(3):
            send(piece, piece, x1_x[j] + k, peers[k])
        send(piece, piece, x1_c[j] + 3, partner)

    def gather_states(j):
        for k in range(3):
            piece = x1_piece(j, wrap(x - k - 1, 4), c)
            arrive(piece, x1_x[j] + k)
            send(piece, piece, x1_c[j] + k, partner)

    def gather_states_wait(j):
        for k in range(3):
            arrive(x1_piece(j, wrap(x - k - 1, 4), other), x1_c[j] + k)
        arrive(x1_piece(j, x, other), x1_c[j] + 3)

    project(0, x0)
    phase_two(1, 1)
    step_states(1)
    phase_two(1, 2)
    arrive(kv.at[0, pl.ds(0, ROWS)], halo_f[0])
    step_states(0)
    gather_states(1)
    phase_two(1, 3)
    gather_states(0)
    gather_states_wait(1)
    gather_states_wait(0)
    phase_two(1, 4)
    project(1, x1)

    out_r = take("r", 2)

    def last_states(j):
        before_states = x1[j * ROWS:(j + 1) * ROWS, pl.ds(own_col, BLK)]
        x2[j * ROWS:(j + 1) * ROWS, :] = (before_states.astype(F32) + attend(1, j)).astype(BF)
        dst = outbuf.at[:, pl.ds(pl.multiple_of(xl * BLK, BLK), BLK)]
        src = x2.at[pl.ds(j * ROWS, ROWS)]
        send(src, dst, out_r + xl, dev(2 * yl + j, dest_y, z, c), away[j])

        @pl.when(home[j])
        def _():
            outbuf[:, pl.ds(pl.multiple_of(xl * BLK, BLK), BLK)] = x2[j * ROWS:(j + 1) * ROWS, :]

    last_states(1)
    arrive(kv.at[1, pl.ds(0, ROWS)], halo_f[1])
    last_states(0)
    for k in range(2):
        arrive(cotg.at[pl.ds(k * ROWS, ROWS)], a2a_c + k, away[k])

    def backward_segment(layer, j, grad_out):
        dq, dk, dv = [], [], []
        for h in range(2):
            cols = slice(h * HEAD, (h + 1) * HEAD)
            vcols = slice(BLK + h * HEAD, BLK + (h + 1) * HEAD)
            queries = q[layer, j * ROWS:(j + 1) * ROWS, cols]
            keys = kv[layer, j * ROWS:(j + 2) * ROWS, cols]
            values = kv[layer, j * ROWS:(j + 2) * ROWS, vcols]
            share = probs[layer, j, h]
            g = grad_out[:, cols]
            dp = nt(g, values)
            wide = share.astype(F32)
            r = jnp.sum(wide * dp, axis=-1, keepdims=True)
            ds = (wide * (dp - r) * SCALE).astype(BF)
            dq.append(nn(ds, keys))
            dk.append(tn(ds, queries))
            dv.append(tn(share, g))
        dqkv[j * ROWS:(j + 1) * ROWS, :BLK] = jnp.concatenate(dq, axis=1).astype(BF)
        return jnp.concatenate(dk + dv, axis=1)

    swap_r = [take("r", 2) for _ in range(LAYERS)]

    def project_back(layer, j):
        rows = slice(j * ROWS, (j + 1) * ROWS)
        lhs = dqkv[rows, :]
        for i in range(2):
            weight = w[layer, 2 * i + other].reshape(512, 3 * BLK)
            swap_send[layer, rows, i * 512:(i + 1) * 512] = nt(lhs, weight).astype(BF)
        src = swap_send.at[layer, pl.ds(j * ROWS, ROWS)]
        send(src, swap_recv.at[layer, pl.ds(j * ROWS, ROWS)], swap_r[layer] + j, partner)
        for i in range(2):
            weight = w[layer, 2 * i + c].reshape(512, 3 * BLK)
            own[rows, i * 512:(i + 1) * 512] = nt(lhs, weight)

    def back_layer(layer, grad_of):
        both = backward_segment(layer, 0, grad_of(0))
        halo_send[layer] = both[:ROWS].astype(BF)
        send(halo_send.at[layer], halo_recv.at[layer], halo_b[layer], group_dev(before))
        rest = both[ROWS:]
        both = backward_segment(layer, 1, grad_of(1))
        dqkv[:ROWS, BLK:] = (rest + both[:ROWS]).astype(BF)
        dkv[...] = both[ROWS:]
        project_back(layer, 0)
        arrive(halo_recv.at[layer], halo_b[layer])
        dqkv[ROWS:, BLK:] = (dkv[...] + halo_recv[layer].astype(F32)).astype(BF)
        project_back(layer, 1)

    back_layer(1, lambda j: cotg[j * ROWS:(j + 1) * ROWS, :])

    rs1_r = [take("r", 3) for _ in range(2)]
    mine = pl.multiple_of(x * BLK, BLK)
    for j in range(2):
        rows = slice(j * ROWS, (j + 1) * ROWS)
        arrive(swap_recv.at[1, pl.ds(j * ROWS, ROWS)], swap_r[1] + j)
        total = own[rows, :] + swap_recv[1, rows, :].astype(F32)
        own[rows, :] = total
        rs_send[1, rows, :] = total.astype(BF)
        for k in range(3):
            col = pl.multiple_of(wrap(x + k + 1, 4) * BLK, BLK)
            src = rs_send.at[1, pl.ds(j * ROWS, ROWS), pl.ds(col, BLK)]
            send(src, rs1_recv.at[k, pl.ds(j * ROWS, ROWS)], rs1_r[j] + k, peers[k])
        g1[rows, :] = cotg[rows, :].astype(F32) + own[rows, pl.ds(mine, BLK)]
    for j in range(2):
        rows = slice(j * ROWS, (j + 1) * ROWS)
        for k in range(3):
            arrive(rs1_recv.at[k, pl.ds(j * ROWS, ROWS)], rs1_r[j] + k)
        g1[rows, :] = (
            g1[rows, :] + rs1_recv[0, rows, :].astype(F32)
            + rs1_recv[1, rows, :].astype(F32) + rs1_recv[2, rows, :].astype(F32)
        )

    back_layer(0, lambda j: g1[j * ROWS:(j + 1) * ROWS, :].astype(BF))

    rs0_r = take("r", 4)
    for j in range(2):
        rows = slice(j * ROWS, (j + 1) * ROWS)
        own[rows, pl.ds(mine, BLK)] = own[rows, pl.ds(mine, BLK)] + g1[rows, :]
        arrive(swap_recv.at[0, pl.ds(j * ROWS, ROWS)], swap_r[0] + j)
        rs_send[0, rows, :] = (own[rows, :] + swap_recv[0, rows, :].astype(F32)).astype(BF)
        for half in range(2):
            src = rs_send.at[0, pl.ds(j * ROWS, ROWS), pl.ds(half * 512, 512)]
            here = (x == 2 * yl + j) & (yl == half)
            send(src, rs0_recv.at[x], rs0_r + x, dev(2 * yl + j, yh * 2 + half, z, c), jnp.logical_not(here))

            @pl.when(here)
            def _():
                rs0_recv[x] = rs_send[0, rows, half * 512:(half + 1) * 512]

    for k in range(2):
        arrive(outbuf.at[:, pl.ds(k * BLK, BLK)], out_r + k, away[k])
    out_ref[...] = outbuf[...]
    total = None
    for k in range(4):
        arrive(rs0_recv.at[k], rs0_r + k, jnp.logical_not(same & (x == k)))
    for k in range(4):
        term = rs0_recv[k].astype(F32)
        total = term if total is None else total + term
    grad_ref[...] = total

    for copy, cond in pending:
        if cond is None:
            copy.wait_send()
        else:
            pl.when(cond)(copy.wait_send)


def per_device(inputs, cotangent, w_query, w_key, w_value, boundary):
    vmem = pl.BlockSpec(memory_space=pltpu.VMEM)
    scratch = [
        ((2, LAYERS, 16, 3 * BLK), BF),
        ((LAYERS, 4, 8, 2, 2, 16, 3 * BLK), BF),
        ((GROUP_ROWS, D), BF),
        ((GROUP_ROWS, D), BF),
        ((GROUP_ROWS, BLK), BF),
        ((LAYERS, 3 * ROWS, 2 * BLK), BF),
        ((LAYERS, GROUP_ROWS, BLK), BF),
        ((LAYERS, 2, 2, ROWS, GROUP_ROWS), BF),
        ((ROWS, 2 * BLK), F32),
        ((LAYERS, ROWS, 2 * BLK), BF),
        ((LAYERS, ROWS, 2 * BLK), BF),
        ((GROUP_ROWS, 3 * BLK), BF),
        ((LAYERS, GROUP_ROWS, 1024), BF),
        ((LAYERS, GROUP_ROWS, 1024), BF),
        ((GROUP_ROWS, 1024), F32),
        ((LAYERS, GROUP_ROWS, 1024), BF),
        ((3, GROUP_ROWS, BLK), BF),
        ((4, ROWS, 512), BF),
        ((GROUP_ROWS, BLK), BF),
        ((ROWS, 512), BF),
        ((GROUP_ROWS, BLK), F32),
    ]
    return pl.pallas_call(
        kernel,
        out_shape=(
            jax.ShapeDtypeStruct((ROWS, 512), BF),
            jax.ShapeDtypeStruct((ROWS, 512), F32),
        ),
        in_specs=[vmem] * 5 + [pl.BlockSpec(memory_space=pltpu.SMEM)],
        out_specs=(vmem, vmem),
        scratch_shapes=[pltpu.VMEM(shape, kind) for shape, kind in scratch]
        + [pltpu.SemaphoreType.DMA((N_SEND,)), pltpu.SemaphoreType.DMA((N_RECV,))],
        compiler_params=pltpu.CompilerParams(
            collective_id=0, has_side_effects=True, vmem_limit_bytes=48 * 1024 * 1024
        ),
    )(inputs, cotangent, w_query, w_key, w_value, boundary)


def solution(mesh):
    return jax.shard_map(
        per_device,
        mesh=mesh,
        in_specs=(
            P("seg", "tp"),
            P("seg", "tp"),
            P(None, "seg", "tp"),
            P(None, "seg", "tp"),
            P(None, "seg", "tp"),
            P(),
        ),
        out_specs=(P("seg", "tp"), P("seg", "tp")),
        check_vma=False,
    )
```

time: 907 us -> 118 us (0.13)
  waiting for transfers between devices: 809 us -> 0 us
  Pallas kernels: 0 us -> 111 us
  matrix products: 29.9 us -> 0 us
  starting transfers between devices: 21.3 us -> 0 us
  between operations: 16 us -> 0.65 us
  blocking collectives: 14 us -> 0 us
    all_gather x6 -> x0, waiting for transfers between devices: 709 us -> none  [the longest x2 245 us: fetch_layer(): lax.all_gather(w_query[layer_id], 'seg', axis=0, tiled=True)]
    pallas_call x0 -> x1, Pallas kernels: none -> 111 us  [per_device(): pl.pallas_call(kernel, out_shape=(jax.ShapeDtypeStruct((ROWS, 512), BF),...]
    reduce_scatter x2 -> x0, waiting for transfers between devices: 72.6 us -> none  [backward_layer(): lax.psum_scatter(partial_value, 'tp', scatter_dimension=1, tiled=True)]
    dot_general x22 -> x0, matrix products: 29 us -> none  [the longest x6 12.2 us: project(): jnp.dot(gathered, weight, preferred_element_type=jnp.float32)]
    ppermute x8 -> x0, waiting for transfers between devices: 25.8 us -> none  [passed_along(): lax.ppermute(value, axis, [(source, source + steps) for source in range(f...]
    ppermute x8 -> x0, starting transfers between devices: 21 us -> none  [passed_along(): lax.ppermute(value, axis, [(source, source + steps) for source in range(f...]
    all_gather x2 -> x0, blocking collectives: 14 us -> none  [forward_layer(): gathered = lax.all_gather(states, 'tp', axis=1, tiled=True)]
  transfers between devices with their start and end apart: 16 -> 0, of which waited for: 14 -> 0; matrix products, arithmetic and copies ran while one was open for 3% -> 0% of each run, Pallas kernels for 0% -> 0%
where the time goes in v1:
time: 118 us
  Pallas kernels  111 us (94%)
  local copies, waits for them, and re-layouts  6.09 us (5%)
    pallas_call x1, Pallas kernels, per_device(): pl.pallas_call(kernel, out_shape=(jax.ShapeDtypeStruct((ROWS, 512), BF),...  111 us
    unnamed x14, local copies, waits for them, and re-layouts  6.09 us

profile of v1, /device:TPU:6, one launch (start us, length us, event | category | flops | bytes accessed | tf_op | source)
XLA Modules:
  0.0 118.0 jit_solution(6307647503508060794)
XLA Ops:
  0.6 0.0 copy-start
  0.6 0.9 copy-done
  1.5 0.0 copy-start.1
  1.5 0.9 copy-done.1
  2.4 0.0 copy-start.2
  2.4 0.8 copy-done.2
  3.2 0.0 copy-start.3
  3.2 0.8 copy-done.3
  4.0 0.0 copy-start.4
  4.0 0.8 copy-done.4
  4.7 0.0 copy-start.5
  4.7 0.7 copy-done.5
  5.4 111.3 %shard_map.77 = (bf16[128,512]{1,0:T(8,128)(2,1)S(1)}, f32[128,512]{1,0:T(8,128)S(1)}) custom-call(bf16[128,512]{1,0:T(8,128)(2,1)S(1)} %copy-done, bf16[128,512]{1,0:T(8,128)(2,1)S(1)} %copy-done.1, bf16[2,16,512]{2,1,0:T(8,128)(2,1)S(1)} %copy-done.2, bf16[2,16,512]{2,1,0:T(8,128)(2,1)S(1)} %copy-done.3, bf16[2,16,512]{2,1,0:T(8,128)(2,1)S(1)} %copy-done.4, ...), custom_call_target="tpu_custom_call" | custom-call | tf_op jit(solution)/shard_map/pallas_call | solution.py:489
  116.7 0.7 copy.10
  117.3 0.7 copy.11
Async XLA Ops:
  0.6 0.9 copy-start
  1.5 0.9 copy-start.1
  2.4 0.8 copy-start.2
  3.2 0.8 copy-start.3
  4.0 0.8 copy-start.4
  4.7 0.7 copy-start.5

commit v2 on v1

--- a/solution.py
+++ b/solution.py
@@ -15,8 +15,9 @@
 GROUP_ROWS = 2 * ROWS
 BLK = 2 * HEAD
 SCALE = 1.0 / math.sqrt(HEAD)
-N_SEND = 176
-N_RECV = 176
+N_LOAD = 15
+N_SEND = 36
+N_RECV = 113
 BF = jnp.bfloat16
 F32 = jnp.float32
 
@@ -34,11 +35,11 @@
 
 
 def kernel(
-    x_in, cot_in, wq, wk, wv, bound,
+    x_hbm, cot_hbm, wq, wk, wv, bound_hbm,
     out_ref, grad_ref,
-    stage, w, x0, x1, cotg, kv, q, probs, dkv, halo_send, halo_recv, dqkv,
+    stage, w, x0, x1, cotg, kv, q, probs, dkv, dkv_last, halo_send, halo_recv, dqkv,
     swap_send, swap_recv, own, rs_send, rs1_recv, rs0_recv, x2, outbuf, g1,
-    ssem, rsem,
+    x_in, cot_in, bound, lsem, ssem, rsem,
 ):
     seg = lax.axis_index("seg")
     tp = lax.axis_index("tp")
@@ -79,31 +80,45 @@
         counts[kind] += n
         return first
 
-    def send(src, dst, recv, target, cond=None):
+    def batch(whole, cond=None):
+        index = take("s")
+        pending.append((whole, index, cond))
+        return index
+
+    def when(cond, action):
+        if cond is None:
+            action()
+        else:
+            pl.when(cond)(action)
+
+    def send(src, dst, recv, target, cond=None, index=None):
         copy = pltpu.make_async_remote_copy(
-            src_ref=src, dst_ref=dst, send_sem=ssem.at[take("s")], recv_sem=rsem.at[recv],
-            device_id=target, device_id_type=MESH,
+            src_ref=src, dst_ref=dst, send_sem=ssem.at[batch(src, cond) if index is None else index],
+            recv_sem=rsem.at[recv], device_id=target, device_id_type=MESH,
         )
-        if cond is None:
-            copy.start()
-        else:
-            pl.when(cond)(copy.start)
-        pending.append((copy, cond))
+        when(cond, copy.start)
 
     def arrive(dst, recv, cond=None):
         copy = pltpu.make_async_remote_copy(
             src_ref=dst, dst_ref=dst, send_sem=ssem.at[0], recv_sem=rsem.at[recv],
             device_id=partner, device_id_type=MESH,
         )
-        if cond is None:
-            copy.wait_recv()
-        else:
-            pl.when(cond)(copy.wait_recv)
+        when(cond, copy.wait_recv)
+
+    loads = []
+
+    def load(src, dst):
+        copy = pltpu.make_async_copy(src, dst, lsem.at[len(loads)])
+        copy.start()
+        loads.append(copy)
 
     for layer in range(LAYERS):
         for j in range(2):
             for t, ref in enumerate((wq, wk, wv)):
-                stage[j, layer, :, t * BLK:(t + 1) * BLK] = ref[layer, :, j * BLK:(j + 1) * BLK]
+                load(ref.at[layer, :, pl.ds(j * BLK, BLK)], stage.at[j, layer, :, pl.ds(t * BLK, BLK)])
+    load(x_hbm, x_in)
+    load(cot_hbm, cot_in)
+    load(bound_hbm, bound)
 
     barrier = pltpu.get_barrier_semaphore()
     known = list(peers) + [partner, group_dev(after), group_dev(before)]
@@ -112,6 +127,8 @@
     known += [dev(x, wrap(y + k, 8), z, c) for k in range(1, 8)]
     for device in known:
         pl.semaphore_signal(barrier, inc=1, device_id=device, device_id_type=MESH)
+    for copy in loads:
+        copy.wait()
     pl.semaphore_wait(barrier, len(known))
 
     same = xh == yl
@@ -140,7 +157,9 @@
     spread_weights(1)
 
     x0_x = [[take("r") for _ in range(2)] for _ in range(2)]
-    x0_c = [[take("r") for _ in range(2)] for _ in range(2)]
+    x0_c = take("r")
+    x0_ring = batch(x0.at[:, pl.ds(0, 1536)], same)
+    x0_pair = batch(x0.at[:, pl.ds(0, 1024)])
     my_rows = pl.multiple_of(xl * ROWS, ROWS)
     my_cols = pl.multiple_of(tp * 512, 512)
 
@@ -156,98 +175,164 @@
     def x0_piece(j, half, core):
         return x0.at[pl.ds(j * ROWS, ROWS), pl.ds(pl.multiple_of(half * 1024 + core * 512, 512), 512)]
 
-    def x0_step(j, half, local):
+    def x0_ring_send(j, half, local):
         piece = x0_piece(j, half, c)
-        here = home[j] & (yl == half)
+        cond = home[j] & ((yl == half) if local else (yl != half))
         if not local:
-            arrive(piece, x0_x[j][half], jnp.logical_not(here))
+            arrive(piece, x0_x[j][half], cond)
         for target in peers:
-            cond = here if local else home[j] & (yl != half)
-            send(piece, piece, x0_x[j][half], target, cond)
+            send(piece, piece, x0_x[j][half], target, cond, x0_ring)
 
     def x0_swap(j, half):
         piece = x0_piece(j, half, c)
-        send(piece, piece, x0_c[j][half], partner)
-
-    for j in range(2):
-        for half in range(2):
-            x0_step(j, half, True)
-
-    for j in range(2):
-        dst = cotg.at[pl.ds(my_rows, ROWS)]
-        src = cot_in.at[:, pl.ds(j * BLK, BLK)]
-        send(src, dst, a2a_c + xl, dev(2 * yl + j, dest_y, z, c), away[j])
-
-        @pl.when(home[j])
-        def _():
-            cotg[pl.ds(my_rows, ROWS)] = cot_in[:, j * BLK:(j + 1) * BLK]
-
-    one = [[take("r", 7) for _ in range(2)] for _ in range(LAYERS)]
+        arrive(piece, x0_x[j][half], away[j])
+        send(piece, piece, x0_c, partner, None, x0_pair)
+
+    def x0_all(action, *rest):
+        for j in range(2):
+            for half in range(2):
+                action(j, half, *rest)
+
+    x0_all(x0_ring_send, True)
+
+    def spread_cotangent():
+        for j in range(2):
+            dst = cotg.at[pl.ds(my_rows, ROWS)]
+            src = cot_in.at[:, pl.ds(j * BLK, BLK)]
+            send(src, dst, a2a_c + xl, dev(2 * yl + j, dest_y, z, c), away[j])
+
+            @pl.when(home[j])
+            def _():
+                cotg[pl.ds(my_rows, ROWS)] = cot_in[:, j * BLK:(j + 1) * BLK]
+
+    out_z = 2 * lax.rem(z, 2) - 1
+    out_y = 2 * yl - 1
+    one = {(kind, rel): take("r") for kind in range(2) for rel in range(4)}
+    direct = [take("r", 7) for _ in range(2)]
+
+    def farthest(s, right):
+        return 4 if (s == 0) == right else 3
+
     two = {
-        (layer, kind, right, s, d): take("r")
-        for layer in range(LAYERS) for d in range(1, 5) for kind in range(2) for right in range(2) for s in range(2)
-        if d <= (4 if right == s else 3)
+        (layer, kind, s, right, d): take("r")
+        for layer in range(LAYERS) for kind in range(2) for s in range(2) for right in (False, True)
+        for d in range(1, farthest(s, right) + 1)
     }
 
-    def phase_one(layer):
-        for k in range(1, 8):
-            a = w.at[layer, yh, z, yl, 0]
-            send(a, a, one[layer][0] + k - 1, dev(x, y, wrap(z + k, 8), c))
-            b = w.at[layer, yh, z, yl, 1]
-            send(b, b, one[layer][1] + k - 1, dev(x, wrap(y + k, 8), z, c))
-
-    def phase_one_wait(layer):
-        for k in range(1, 8):
-            arrive(w.at[layer, yh, wrap(z - k, 8), yl, 0], one[layer][0] + k - 1)
-            ys = wrap(y - k, 8)
-            arrive(w.at[layer, lax.div(ys, 2), z, lax.rem(ys, 2), 1], one[layer][1] + k - 1)
-
-    def chunk(layer, kind, right, s, d):
+    next_to = [
+        {k: dev(x, y, wrap(z + k, 8), c) for k in (1, -1)},
+        {k: dev(x, wrap(y + k, 8), z, c) for k in (1, -1)},
+    ]
+    outer = [dev(x, y, wrap(z + out_z, 8), c), dev(x, wrap(y + out_y, 8), z, c)]
+    mate = [dev(x, y, z - out_z, c), dev(x, y - out_y, z, c)]
+    z_at = {k: wrap(z + k, 8) for k in range(-4, 5)}
+    y_at = {k: (lax.div(wrap(y + k, 8), 2), lax.rem(wrap(y + k, 8), 2)) for k in range(-4, 5)}
+    z_pair = lax.div(z, 2)
+    pairs = [
+        [z_pair * 2] + [wrap(z_pair + k, 4) * 2 for k in (out_z, -out_z, 2)],
+        [yh] + [wrap(yh + k, 4) for k in (out_y, -out_y, 2)],
+    ]
+
+    def block(layer, kind, at_mate):
         if kind == 0:
-            ys = wrap(y - d if right else y + d, 8)
-            return w.at[layer, lax.div(ys, 2), pl.ds(4 * s, 4), lax.rem(ys, 2), 0]
-        zs = wrap(z - d if right else z + d, 8)
-        return w.at[layer, pl.ds(2 * s, 2), zs, :, 1]
-
-    def forward(layer, kind, right, s, d):
-        step = 1 if right else -1
-        target = dev(x, wrap(y + step, 8), z, c) if kind == 0 else dev(x, y, wrap(z + step, 8), c)
-        piece = chunk(layer, kind, right, s, d)
-        send(piece, piece, two[layer, kind, right, s, d + 1], target)
-
-    def phase_two(layer, d):
-        for s in range(2):
+            return w.at[layer, yh, z - out_z if at_mate else z, yl, 0]
+        return w.at[layer, yh, z, 1 - yl if at_mate else yl, 1]
+
+    def pair(layer, kind, rel, shift):
+        if kind == 0:
+            at = y_at[shift]
+            return w.at[layer, at[0], pl.ds(pairs[0][rel], 2), at[1], 0]
+        return w.at[layer, pairs[1][rel], z_at[shift], :, 1]
+
+    def part(layer, kind, s, shift):
+        if kind == 0:
+            return w.at[layer, y_at[shift][0], pl.ds(4 * s, 4), y_at[shift][1], 0]
+        return w.at[layer, pl.ds(2 * s, 2), z_at[shift], :, 1]
+
+    batch_one = [[batch(w.at[layer, 0, pl.ds(0, 7), 0, 0]) for _ in range(2)] for layer in range(LAYERS)]
+    batch_two = {
+        (layer, kind, s): batch(w.at[layer, :, pl.ds(0, 6 if layer + kind + s == 0 else 7), 0, 0])
+        for layer in range(LAYERS) for kind in range(2) for s in range(2)
+    }
+    lead = take("s")
+
+    def pass_on(layer, kind, s, right, d):
+        if d < farthest(s, right):
+            piece = part(layer, kind, s, 0 if d == 0 else (-d if right else d))
+            index = lead if right and layer + kind + s + d == 0 else batch_two[layer, kind, s]
+            send(piece, piece, two[layer, kind, s, right, d + 1], next_to[1 - kind][1 if right else -1], None, index)
+
+    def ring(layer, s, d):
+        for kind in range(2):
+            for right in (False, True):
+                if 1 <= d <= farthest(s, right):
+                    arrive(part(layer, kind, s, -d if right else d), two[layer, kind, s, right, d])
+                if d <= farthest(s, right):
+                    pass_on(layer, kind, s, right, d)
+
+    def block_from(kind, k):
+        if kind == 0:
+            return w.at[0, yh, z_at[-k], yl, 0]
+        return w.at[0, y_at[-k][0], z, y_at[-k][1], 1]
+
+    def direct_send():
+        for k in (1, -1, 2, -2, 3, -3, 4):
             for kind in range(2):
-                for right in range(2):
-                    most = 4 if right == s else 3
-                    if d > most:
-                        continue
-                    if d > 0:
-                        arrive(chunk(layer, kind, right, s, d), two[layer, kind, right, s, d])
-                    if d < most:
-                        forward(layer, kind, right, s, d)
+                mine = block(0, kind, False)
+                to = wrap((z if kind == 0 else y) + k, 8)
+                target = dev(x, y, to, c) if kind == 0 else dev(x, to, z, c)
+                send(mine, mine, direct[kind] + k + 3 - (k > 0), target, None, batch_one[0][kind])
+
+    def direct_wait():
+        for k in (1, -1, 2, -2, 3, -3, 4):
+            for kind in range(2):
+                arrive(block_from(kind, k), direct[kind] + k + 3 - (k > 0))
+
+    def relay(t):
+        for kind in range(2):
+            if t == 0:
+                mine = block(1, kind, False)
+                send(mine, mine, one[kind, 0], mate[kind], None, batch_one[1][kind])
+                continue
+            rel = t - 1
+            if rel == 0:
+                arrive(block(1, kind, True), one[kind, 0])
+            else:
+                arrive(pair(1, kind, rel, 0), one[kind, rel])
+            if rel < 3:
+                piece = pair(1, kind, rel, 0)
+                send(piece, piece, one[kind, rel + 1], (mate if rel == 1 else outer)[kind], None, batch_one[1][kind])
 
     spread_weights_wait(0)
-    phase_one(0)
+    direct_send()
     spread_weights_wait(1)
-    phase_one_wait(0)
-    phase_two(0, 0)
-    phase_one(1)
-    for j in range(2):
-        for half in range(2):
-            x0_step(j, half, False)
-    phase_two(0, 1)
-    for j in range(2):
-        for half in range(2):
-            x0_swap(j, half)
-    phase_two(0, 2)
-    phase_two(0, 3)
-    phase_one_wait(1)
-    phase_two(1, 0)
-    phase_two(0, 4)
-    for j in range(2):
-        for half in range(2):
-            arrive(x0_piece(j, half, other), x0_c[j][half])
+    relay(0)
+    direct_wait()
+    ring(0, 0, 0)
+    x0_all(x0_ring_send, False)
+    relay(1)
+    head = part(0, 0, 0, 0)
+    pltpu.make_async_remote_copy(
+        src_ref=head, dst_ref=head, send_sem=ssem.at[lead], recv_sem=rsem.at[0],
+        device_id=partner, device_id_type=MESH,
+    ).wait_send()
+    ring(0, 1, 0)
+    ring(0, 0, 1)
+    relay(2)
+    ring(0, 1, 1)
+    relay(3)
+    ring(0, 0, 2)
+    relay(4)
+    ring(0, 1, 2)
+    x0_all(x0_swap)
+    ring(0, 0, 3)
+    ring(1, 0, 0)
+    ring(0, 1, 3)
+    ring(1, 1, 0)
+    spread_cotangent()
+    ring(0, 0, 4)
+    ring(0, 1, 4)
+    arrive(x0.at[:, pl.ds(0, 1024)], x0_c)
 
     pos_q = lax.broadcasted_iota(jnp.int32, (ROWS, GROUP_ROWS), 0)
     pos_k = lax.broadcasted_iota(jnp.int32, (ROWS, GROUP_ROWS), 1)
@@ -299,7 +384,8 @@
         return x1.at[pl.ds(j * ROWS, ROWS), pl.ds(pl.multiple_of(col, BLK), BLK)]
 
     x1_x = [take("r", 3) for _ in range(2)]
-    x1_c = [take("r", 4) for _ in range(2)]
+    x1_c = take("r", 2)
+    x1_sent = batch(x1.at[:, pl.ds(0, 1792)])
 
     def step_states(j):
         before_states = x0[j * ROWS:(j + 1) * ROWS, pl.ds(own_col, BLK)]
@@ -308,32 +394,34 @@
         ).astype(BF)
         piece = x1_piece(j, x, c)
         for k in range(3):
-            send(piece, piece, x1_x[j] + k, peers[k])
-        send(piece, piece, x1_c[j] + 3, partner)
+            send(piece, piece, x1_x[j] + k, peers[k], None, x1_sent)
+        send(piece, piece, x1_c + j, partner, None, x1_sent)
 
     def gather_states(j):
         for k in range(3):
             piece = x1_piece(j, wrap(x - k - 1, 4), c)
             arrive(piece, x1_x[j] + k)
-            send(piece, piece, x1_c[j] + k, partner)
+            send(piece, piece, x1_c + j, partner, None, x1_sent)
 
     def gather_states_wait(j):
-        for k in range(3):
-            arrive(x1_piece(j, wrap(x - k - 1, 4), other), x1_c[j] + k)
-        arrive(x1_piece(j, x, other), x1_c[j] + 3)
+        arrive(x1.at[pl.ds(j * ROWS, ROWS), pl.ds(0, 1024)], x1_c + j)
 
     project(0, x0)
-    phase_two(1, 1)
+    ring(1, 0, 1)
     step_states(1)
-    phase_two(1, 2)
+    ring(1, 1, 1)
     arrive(kv.at[0, pl.ds(0, ROWS)], halo_f[0])
     step_states(0)
+    ring(1, 0, 2)
     gather_states(1)
-    phase_two(1, 3)
+    ring(1, 1, 2)
     gather_states(0)
+    ring(1, 0, 3)
+    ring(1, 1, 3)
     gather_states_wait(1)
     gather_states_wait(0)
-    phase_two(1, 4)
+    ring(1, 0, 4)
+    ring(1, 1, 4)
     project(1, x1)
 
     out_r = take("r", 2)
@@ -348,12 +436,6 @@
         @pl.when(home[j])
         def _():
             outbuf[:, pl.ds(pl.multiple_of(xl * BLK, BLK), BLK)] = x2[j * ROWS:(j + 1) * ROWS, :]
-
-    last_states(1)
-    arrive(kv.at[1, pl.ds(0, ROWS)], halo_f[1])
-    last_states(0)
-    for k in range(2):
-        arrive(cotg.at[pl.ds(k * ROWS, ROWS)], a2a_c + k, away[k])
 
     def backward_segment(layer, j, grad_out):
         dq, dk, dv = [], [], []
@@ -376,6 +458,7 @@
         return jnp.concatenate(dk + dv, axis=1)
 
     swap_r = [take("r", 2) for _ in range(LAYERS)]
+    swap_sent = [batch(swap_send.at[layer]) for layer in range(LAYERS)]
 
     def project_back(layer, j):
         rows = slice(j * ROWS, (j + 1) * ROWS)
@@ -384,27 +467,40 @@
             weight = w[layer, 2 * i + other].reshape(512, 3 * BLK)
             swap_send[layer, rows, i * 512:(i + 1) * 512] = nt(lhs, weight).astype(BF)
         src = swap_send.at[layer, pl.ds(j * ROWS, ROWS)]
-        send(src, swap_recv.at[layer, pl.ds(j * ROWS, ROWS)], swap_r[layer] + j, partner)
+        send(src, swap_recv.at[layer, pl.ds(j * ROWS, ROWS)], swap_r[layer] + j, partner, None, swap_sent[layer])
         for i in range(2):
             weight = w[layer, 2 * i + c].reshape(512, 3 * BLK)
             own[rows, i * 512:(i + 1) * 512] = nt(lhs, weight)
 
-    def back_layer(layer, grad_of):
-        both = backward_segment(layer, 0, grad_of(0))
+    def back_first(layer, grad):
+        both = backward_segment(layer, 0, grad)
         halo_send[layer] = both[:ROWS].astype(BF)
         send(halo_send.at[layer], halo_recv.at[layer], halo_b[layer], group_dev(before))
-        rest = both[ROWS:]
-        both = backward_segment(layer, 1, grad_of(1))
-        dqkv[:ROWS, BLK:] = (rest + both[:ROWS]).astype(BF)
-        dkv[...] = both[ROWS:]
+        dkv[:ROWS, :] = both[ROWS:]
+
+    def back_second(layer, grad):
+        both = backward_segment(layer, 1, grad)
+        dkv[ROWS:, :] = both[:ROWS]
+        dkv_last[...] = both[ROWS:]
+
+    def back_finish(layer):
+        dqkv[:ROWS, BLK:] = (dkv[:ROWS, :] + dkv[ROWS:, :]).astype(BF)
         project_back(layer, 0)
         arrive(halo_recv.at[layer], halo_b[layer])
-        dqkv[ROWS:, BLK:] = (dkv[...] + halo_recv[layer].astype(F32)).astype(BF)
+        dqkv[ROWS:, BLK:] = (dkv_last[...] + halo_recv[layer].astype(F32)).astype(BF)
         project_back(layer, 1)
 
-    back_layer(1, lambda j: cotg[j * ROWS:(j + 1) * ROWS, :])
-
-    rs1_r = [take("r", 3) for _ in range(2)]
+    last_states(1)
+    for k in range(2):
+        arrive(cotg.at[pl.ds(k * ROWS, ROWS)], a2a_c + k, away[k])
+    back_second(1, cotg[ROWS:, :])
+    arrive(kv.at[1, pl.ds(0, ROWS)], halo_f[1])
+    last_states(0)
+    back_first(1, cotg[:ROWS, :])
+    back_finish(1)
+
+    rs1_r = take("r", 2)
+    rs1_sent = batch(rs_send.at[1, :, pl.ds(0, 768)])
     mine = pl.multiple_of(x * BLK, BLK)
     for j in range(2):
         rows = slice(j * ROWS, (j + 1) * ROWS)
@@ -415,18 +511,19 @@
         for k in range(3):
             col = pl.multiple_of(wrap(x + k + 1, 4) * BLK, BLK)
             src = rs_send.at[1, pl.ds(j * ROWS, ROWS), pl.ds(col, BLK)]
-            send(src, rs1_recv.at[k, pl.ds(j * ROWS, ROWS)], rs1_r[j] + k, peers[k])
+            send(src, rs1_recv.at[k, pl.ds(j * ROWS, ROWS)], rs1_r + j, peers[k], None, rs1_sent)
         g1[rows, :] = cotg[rows, :].astype(F32) + own[rows, pl.ds(mine, BLK)]
     for j in range(2):
         rows = slice(j * ROWS, (j + 1) * ROWS)
-        for k in range(3):
-            arrive(rs1_recv.at[k, pl.ds(j * ROWS, ROWS)], rs1_r[j] + k)
+        arrive(rs1_recv.at[:, pl.ds(j * ROWS, ROWS)], rs1_r + j)
         g1[rows, :] = (
             g1[rows, :] + rs1_recv[0, rows, :].astype(F32)
             + rs1_recv[1, rows, :].astype(F32) + rs1_recv[2, rows, :].astype(F32)
         )
 
-    back_layer(0, lambda j: g1[j * ROWS:(j + 1) * ROWS, :].astype(BF))
+    back_first(0, g1[:ROWS, :].astype(BF))
+    back_second(0, g1[ROWS:, :].astype(BF))
+    back_finish(0)
 
     rs0_r = take("r", 4)
     for j in range(2):
@@ -454,11 +551,14 @@
         total = term if total is None else total + term
     grad_ref[...] = total
 
-    for copy, cond in pending:
-        if cond is None:
-            copy.wait_send()
-        else:
-            pl.when(cond)(copy.wait_send)
+    for whole, index, cond in pending:
+        copy = pltpu.make_async_remote_copy(
+            src_ref=whole, dst_ref=whole, send_sem=ssem.at[index], recv_sem=rsem.at[0],
+            device_id=partner, device_id_type=MESH,
+        )
+        when(cond, copy.wait_send)
+
+    assert counts["s"] <= N_SEND and counts["r"] <= N_RECV, counts
 
 
 def per_device(inputs, cotangent, w_query, w_key, w_value, boundary):
@@ -472,6 +572,7 @@
         ((LAYERS, 3 * ROWS, 2 * BLK), BF),
         ((LAYERS, GROUP_ROWS, BLK), BF),
         ((LAYERS, 2, 2, ROWS, GROUP_ROWS), BF),
+        ((GROUP_ROWS, 2 * BLK), F32),
         ((ROWS, 2 * BLK), F32),
         ((LAYERS, ROWS, 2 * BLK), BF),
         ((LAYERS, ROWS, 2 * BLK), BF),
@@ -492,12 +593,18 @@
             jax.ShapeDtypeStruct((ROWS, 512), BF),
             jax.ShapeDtypeStruct((ROWS, 512), F32),
         ),
-        in_specs=[vmem] * 5 + [pl.BlockSpec(memory_space=pltpu.SMEM)],
+        in_specs=[pl.BlockSpec(memory_space=pl.ANY)] * 6,
         out_specs=(vmem, vmem),
         scratch_shapes=[pltpu.VMEM(shape, kind) for shape, kind in scratch]
-        + [pltpu.SemaphoreType.DMA((N_SEND,)), pltpu.SemaphoreType.DMA((N_RECV,))],
+        + [
+            pltpu.VMEM((ROWS, 512), BF),
+            pltpu.VMEM((ROWS, 512), BF),
+            pltpu.SMEM((ROWS,), jnp.int32),
+            pltpu.SemaphoreType.DMA((N_LOAD,)),
+            pltpu.SemaphoreType.DMA((N_SEND,)), pltpu.SemaphoreType.DMA((N_RECV,)),
+        ],
         compiler_params=pltpu.CompilerParams(
-            collective_id=0, has_side_effects=True, vmem_limit_bytes=48 * 1024 * 1024
+            collective_id=0, has_side_effects=True, vmem_limit_bytes=60 * 1024 * 1024
         ),
     )(inputs, cotangent, w_query, w_key, w_value, boundary)
 

time: 118 us -> 109 us (0.924)
  Pallas kernels: 111 us -> 106 us
  local copies, waits for them, and re-layouts: 6.09 us -> 2.32 us
    pallas_call x1, Pallas kernels: 111 us -> 106 us  [per_device(): pl.pallas_call(kernel, out_shape=(jax.ShapeDtypeStruct((ROWS, 512), BF),...]
    unnamed x14 -> x4, local copies, waits for them, and re-layouts: 6.09 us -> 2.32 us
where the time goes in v2:
time: 109 us
  Pallas kernels  106 us (97%)
  local copies, waits for them, and re-layouts  2.32 us (2%)
    pallas_call x1, Pallas kernels, per_device(): pl.pallas_call(kernel, out_shape=(jax.ShapeDtypeStruct((ROWS, 512), BF),...  106 us
    unnamed x4, local copies, waits for them, and re-layouts  2.32 us

profile of v2, /device:TPU:6, one launch (start us, length us, event | category | flops | bytes accessed | tf_op | source)
XLA Modules:
  0.0 108.9 jit_solution(3235667052875392039)
XLA Ops:
  0.6 105.9 %shard_map.77 = (bf16[128,512]{1,0:T(8,128)(2,1)}, f32[128,512]{1,0:T(8,128)}) custom-call(bf16[128,512]{1,0:T(8,128)(2,1)} %x_hbm.1, bf16[128,512]{1,0:T(8,128)(2,1)} %cot_hbm.1, bf16[2,16,512]{2,1,0:T(8,128)(2,1)} %wq.1, bf16[2,16,512]{2,1,0:T(8,128)(2,1)} %wk.1, bf16[2,16,512]{2,1,0:T(8,128)(2,1)} %wv.1, s32[128]{0:T(128)} %bound_hbm.1), custom_call_target="tpu_custom_call" | custom-call | tf_op jit(solution)/shard_map/pallas_call | solution.py:590
  106.6 0.0 copy-start
  106.6 1.6 %copy.10 = bf16[128,512]{1,0:T(8,128)(2,1)} copy(bf16[128,512]{1,0:T(8,128)(2,1)} %get-tuple-element.4) | data formatting | bytes 262144
  108.2 0.0 copy-done
  108.2 0.7 copy.11
Async XLA Ops:
  106.6 1.6 %copy-start = (f32[128,512]{1,0:T(8,128)S(1)}, f32[128,512]{1,0:T(8,128)}, u32[]{:S(2)}) copy-start(f32[128,512]{1,0:T(8,128)} %get-tuple-element.5) | copy-start | bytes 786436

commit v3 on v2

--- a/solution.py
+++ b/solution.py
@@ -483,9 +483,53 @@
         dkv[ROWS:, :] = both[:ROWS]
         dkv_last[...] = both[ROWS:]
 
-    def back_finish(layer):
+    rs1_r = take("r", 2)
+    rs1_sent = batch(rs_send.at[1, :, pl.ds(0, 768)])
+    rs0_r = take("r", 4)
+    mine = pl.multiple_of(x * BLK, BLK)
+
+    def swapped(layer, j):
+        rows = slice(j * ROWS, (j + 1) * ROWS)
+        arrive(swap_recv.at[layer, pl.ds(j * ROWS, ROWS)], swap_r[layer] + j)
+        return own[rows, :] + swap_recv[layer, rows, :].astype(F32)
+
+    def sum_one(j):
+        rows = slice(j * ROWS, (j + 1) * ROWS)
+        total = swapped(1, j)
+        own[rows, :] = total
+        rs_send[1, rows, :] = total.astype(BF)
+        for k in range(3):
+            col = pl.multiple_of(wrap(x + k + 1, 4) * BLK, BLK)
+            src = rs_send.at[1, pl.ds(j * ROWS, ROWS), pl.ds(col, BLK)]
+            send(src, rs1_recv.at[k, pl.ds(j * ROWS, ROWS)], rs1_r + j, peers[k], None, rs1_sent)
+        g1[rows, :] = cotg[rows, :].astype(F32) + own[rows, pl.ds(mine, BLK)]
+
+    def summed_one(j):
+        rows = slice(j * ROWS, (j + 1) * ROWS)
+        arrive(rs1_recv.at[:, pl.ds(j * ROWS, ROWS)], rs1_r + j)
+        g1[rows, :] = (
+            g1[rows, :] + rs1_recv[0, rows, :].astype(F32)
+            + rs1_recv[1, rows, :].astype(F32) + rs1_recv[2, rows, :].astype(F32)
+        )
+
+    def sum_last(j):
+        rows = slice(j * ROWS, (j + 1) * ROWS)
+        own[rows, pl.ds(mine, BLK)] = own[rows, pl.ds(mine, BLK)] + g1[rows, :]
+        rs_send[0, rows, :] = swapped(0, j).astype(BF)
+        for half in range(2):
+            src = rs_send.at[0, pl.ds(j * ROWS, ROWS), pl.ds(half * 512, 512)]
+            here = (x == 2 * yl + j) & (yl == half)
+            send(src, rs0_recv.at[x], rs0_r + x, dev(2 * yl + j, yh * 2 + half, z, c), jnp.logical_not(here))
+
+            @pl.when(here)
+            def _():
+                rs0_recv[x] = rs_send[0, rows, half * 512:(half + 1) * 512]
+
+    def back_own(layer):
         dqkv[:ROWS, BLK:] = (dkv[:ROWS, :] + dkv[ROWS:, :]).astype(BF)
         project_back(layer, 0)
+
+    def back_halo(layer):
         arrive(halo_recv.at[layer], halo_b[layer])
         dqkv[ROWS:, BLK:] = (dkv_last[...] + halo_recv[layer].astype(F32)).astype(BF)
         project_back(layer, 1)
@@ -497,48 +541,18 @@
     arrive(kv.at[1, pl.ds(0, ROWS)], halo_f[1])
     last_states(0)
     back_first(1, cotg[:ROWS, :])
-    back_finish(1)
-
-    rs1_r = take("r", 2)
-    rs1_sent = batch(rs_send.at[1, :, pl.ds(0, 768)])
-    mine = pl.multiple_of(x * BLK, BLK)
-    for j in range(2):
-        rows = slice(j * ROWS, (j + 1) * ROWS)
-        arrive(swap_recv.at[1, pl.ds(j * ROWS, ROWS)], swap_r[1] + j)
-        total = own[rows, :] + swap_recv[1, rows, :].astype(F32)
-        own[rows, :] = total
-        rs_send[1, rows, :] = total.astype(BF)
-        for k in range(3):
-            col = pl.multiple_of(wrap(x + k + 1, 4) * BLK, BLK)
-            src = rs_send.at[1, pl.ds(j * ROWS, ROWS), pl.ds(col, BLK)]
-            send(src, rs1_recv.at[k, pl.ds(j * ROWS, ROWS)], rs1_r + j, peers[k], None, rs1_sent)
-        g1[rows, :] = cotg[rows, :].astype(F32) + own[rows, pl.ds(mine, BLK)]
-    for j in range(2):
-        rows = slice(j * ROWS, (j + 1) * ROWS)
-        arrive(rs1_recv.at[:, pl.ds(j * ROWS, ROWS)], rs1_r + j)
-        g1[rows, :] = (
-            g1[rows, :] + rs1_recv[0, rows, :].astype(F32)
-            + rs1_recv[1, rows, :].astype(F32) + rs1_recv[2, rows, :].astype(F32)
-        )
-
+    back_own(1)
+    sum_one(0)
+    back_halo(1)
+    sum_one(1)
+    summed_one(0)
     back_first(0, g1[:ROWS, :].astype(BF))
+    summed_one(1)
     back_second(0, g1[ROWS:, :].astype(BF))
-    back_finish(0)
-
-    rs0_r = take("r", 4)
-    for j in range(2):
-        rows = slice(j * ROWS, (j + 1) * ROWS)
-        own[rows, pl.ds(mine, BLK)] = own[rows, pl.ds(mine, BLK)] + g1[rows, :]
-        arrive(swap_recv.at[0, pl.ds(j * ROWS, ROWS)], swap_r[0] + j)
-        rs_send[0, rows, :] = (own[rows, :] + swap_recv[0, rows, :].astype(F32)).astype(BF)
-        for half in range(2):
-            src = rs_send.at[0, pl.ds(j * ROWS, ROWS), pl.ds(half * 512, 512)]
-            here = (x == 2 * yl + j) & (yl == half)
-            send(src, rs0_recv.at[x], rs0_r + x, dev(2 * yl + j, yh * 2 + half, z, c), jnp.logical_not(here))
-
-            @pl.when(here)
-            def _():
-                rs0_recv[x] = rs_send[0, rows, half * 512:(half + 1) * 512]
+    back_own(0)
+    back_halo(0)
+    sum_last(0)
+    sum_last(1)
 
     for k in range(2):
         arrive(outbuf.at[:, pl.ds(k * BLK, BLK)], out_r + k, away[k])

time: 109 us -> 107 us (0.982)
  Pallas kernels: 106 us -> 104 us
    pallas_call x1, Pallas kernels: 106 us -> 104 us  [per_device(): pl.pallas_call(kernel, out_shape=(jax.ShapeDtypeStruct((ROWS, 512), BF),...]
where the time goes in v3:
time: 107 us
  Pallas kernels  104 us (97%)
  local copies, waits for them, and re-layouts  2.32 us (2%)
    pallas_call x1, Pallas kernels, per_device(): pl.pallas_call(kernel, out_shape=(jax.ShapeDtypeStruct((ROWS, 512), BF),...  104 us
    unnamed x4, local copies, waits for them, and re-layouts  2.32 us

profile of v3, /device:TPU:6, one launch (start us, length us, event | category | flops | bytes accessed | tf_op | source)
XLA Modules:
  0.0 107.2 jit_solution(12591432707188205881)
XLA Ops:
  0.6 104.2 %shard_map.77 = (bf16[128,512]{1,0:T(8,128)(2,1)}, f32[128,512]{1,0:T(8,128)}) custom-call(bf16[128,512]{1,0:T(8,128)(2,1)} %x_hbm.1, bf16[128,512]{1,0:T(8,128)(2,1)} %cot_hbm.1, bf16[2,16,512]{2,1,0:T(8,128)(2,1)} %wq.1, bf16[2,16,512]{2,1,0:T(8,128)(2,1)} %wk.1, bf16[2,16,512]{2,1,0:T(8,128)(2,1)} %wv.1, s32[128]{0:T(128)} %bound_hbm.1), custom_call_target="tpu_custom_call" | custom-call | tf_op jit(solution)/shard_map/pallas_call | solution.py:604
  104.8 0.0 copy-start
  104.8 1.6 %copy.10 = bf16[128,512]{1,0:T(8,128)(2,1)} copy(bf16[128,512]{1,0:T(8,128)(2,1)} %get-tuple-element.4) | data formatting | bytes 262144
  106.4 0.0 copy-done
  106.4 0.7 copy.11
Async XLA Ops:
  104.8 1.6 %copy-start = (f32[128,512]{1,0:T(8,128)S(1)}, f32[128,512]{1,0:T(8,128)}, u32[]{:S(2)}) copy-start(f32[128,512]{1,0:T(8,128)} %get-tuple-element.5) | copy-start | bytes 786436

commit v4 on v3

--- a/solution.py
+++ b/solution.py
@@ -17,7 +17,7 @@
 SCALE = 1.0 / math.sqrt(HEAD)
 N_LOAD = 15
 N_SEND = 36
-N_RECV = 113
+N_RECV = 117
 BF = jnp.bfloat16
 F32 = jnp.float32
 
@@ -158,22 +158,25 @@
 
     x0_x = [[take("r") for _ in range(2)] for _ in range(2)]
     x0_c = take("r")
-    x0_ring = batch(x0.at[:, pl.ds(0, 1536)], same)
-    x0_pair = batch(x0.at[:, pl.ds(0, 1024)])
+    x0_ring = batch(x0.at[pl.ds(0, GROUP_ROWS), pl.ds(0, 1536)], same)
+    x0_pair = batch(x0.at[pl.ds(0, GROUP_ROWS), pl.ds(0, 1024)])
+    last_r, last_x, last_c = take("r", LAYERS), take("r", LAYERS), take("r", LAYERS)
+    last_sent = [batch(x0.at[pl.ds(0, GROUP_ROWS), pl.ds(0, 1024)]) for _ in range(LAYERS)]
+    states_of = (x0, x1)
     my_rows = pl.multiple_of(xl * ROWS, ROWS)
     my_cols = pl.multiple_of(tp * 512, 512)
 
     @pl.when(same)
     def _():
-        x0[pl.ds(my_rows, ROWS), pl.ds(my_cols, 512)] = x_in[...]
+        x0[pl.ds(ROWS + my_rows, ROWS), pl.ds(my_cols, 512)] = x_in[...]
 
     send(
-        x_in, x0.at[pl.ds(my_rows, ROWS), pl.ds(my_cols, 512)], x0_x[0][0] + xl * 2 + yl,
+        x_in, x0.at[pl.ds(ROWS + my_rows, ROWS), pl.ds(my_cols, 512)], x0_x[0][0] + xl * 2 + yl,
         dev(x, pair_y, z, c), jnp.logical_not(same),
     )
 
     def x0_piece(j, half, core):
-        return x0.at[pl.ds(j * ROWS, ROWS), pl.ds(pl.multiple_of(half * 1024 + core * 512, 512), 512)]
+        return x0.at[pl.ds((j + 1) * ROWS, ROWS), pl.ds(pl.multiple_of(half * 1024 + core * 512, 512), 512)]
 
     def x0_ring_send(j, half, local):
         piece = x0_piece(j, half, c)
@@ -194,6 +197,30 @@
                 action(j, half, *rest)
 
     x0_all(x0_ring_send, True)
+
+    def quarter(layer, row, xs, core):
+        col = lax.div(xs, 2) * 1024 + core * 512 + lax.rem(xs, 2) * BLK
+        return states_of[layer].at[pl.ds(row, ROWS), pl.ds(pl.multiple_of(col, BLK), BLK)]
+
+    def last_send(layer):
+        piece, dst = quarter(layer, 2 * ROWS, x, c), quarter(layer, 0, x, c)
+        send(piece, dst, last_r + layer, group_dev(after), None, last_sent[layer])
+
+    def last_spread(layer):
+        piece = quarter(layer, 0, x, c)
+        arrive(piece, last_r + layer)
+        for target in peers:
+            send(piece, piece, last_x + layer, target, None, last_sent[layer])
+        send(piece, piece, last_c + layer, partner, None, last_sent[layer])
+
+    def last_swap(layer):
+        arrive(states_of[layer].at[pl.ds(0, ROWS), pl.ds(0, 768)], last_x + layer)
+        for k in range(3):
+            piece = quarter(layer, 0, wrap(x - k - 1, 4), c)
+            send(piece, piece, last_c + layer, partner, None, last_sent[layer])
+
+    def last_wait(layer):
+        arrive(states_of[layer].at[pl.ds(0, ROWS), pl.ds(0, 1024)], last_c + layer)
 
     def spread_cotangent():
         for j in range(2):
@@ -319,20 +346,24 @@
     ring(0, 1, 0)
     ring(0, 0, 1)
     relay(2)
+    x0_all(x0_swap)
+    last_send(0)
     ring(0, 1, 1)
     relay(3)
     ring(0, 0, 2)
     relay(4)
     ring(0, 1, 2)
-    x0_all(x0_swap)
+    last_spread(0)
     ring(0, 0, 3)
     ring(1, 0, 0)
     ring(0, 1, 3)
     ring(1, 1, 0)
+    last_swap(0)
     spread_cotangent()
     ring(0, 0, 4)
     ring(0, 1, 4)
-    arrive(x0.at[:, pl.ds(0, 1024)], x0_c)
+    arrive(x0.at[pl.ds(0, GROUP_ROWS), pl.ds(0, 1024)], x0_c)
+    last_wait(0)
 
     pos_q = lax.broadcasted_iota(jnp.int32, (ROWS, GROUP_ROWS), 0)
     pos_k = lax.broadcasted_iota(jnp.int32, (ROWS, GROUP_ROWS), 1)
@@ -348,20 +379,20 @@
         segment = (pos_m >= 0) & (pos_m <= pos_q) & ((pos_m >= now) | (pos_q < now))
         return memory | segment
 
-    halo_f = [take("r") for _ in range(LAYERS)]
     halo_b = [take("r") for _ in range(LAYERS)]
 
     def project(layer, states):
-        total = None
-        for part in range(4):
-            weight = w[layer, part].reshape(512, 3 * BLK)
-            term = nn(states[:, part * 512:(part + 1) * 512], weight)
-            total = term if total is None else total + term
-        total = total.astype(BF)
-        q[layer] = total[:, :BLK]
-        kv[layer, ROWS:, :] = total[:, BLK:]
-        tail = kv.at[layer, pl.ds(2 * ROWS, ROWS)]
-        send(tail, kv.at[layer, pl.ds(0, ROWS)], halo_f[layer], group_dev(after))
+        def columns(first, last):
+            total = None
+            for part in range(4):
+                weight = w[layer, part].reshape(512, 3 * BLK)[:, first:last]
+                rows = slice(0 if first else ROWS, None)
+                term = nn(states[rows, part * 512:(part + 1) * 512], weight)
+                total = term if total is None else total + term
+            return total.astype(BF)
+
+        kv[layer] = columns(BLK, 3 * BLK)
+        q[layer] = columns(0, BLK)
 
     def attend(layer, j):
         visible = mask(j)
@@ -380,16 +411,15 @@
         return jnp.concatenate(results, axis=1)
 
     def x1_piece(j, xs, core):
-        col = lax.div(xs, 2) * 1024 + core * 512 + lax.rem(xs, 2) * BLK
-        return x1.at[pl.ds(j * ROWS, ROWS), pl.ds(pl.multiple_of(col, BLK), BLK)]
+        return quarter(1, (j + 1) * ROWS, xs, core)
 
     x1_x = [take("r", 3) for _ in range(2)]
     x1_c = take("r", 2)
-    x1_sent = batch(x1.at[:, pl.ds(0, 1792)])
+    x1_sent = batch(x1.at[pl.ds(0, GROUP_ROWS), pl.ds(0, 1792)])
 
     def step_states(j):
-        before_states = x0[j * ROWS:(j + 1) * ROWS, pl.ds(own_col, BLK)]
-        x1[j * ROWS:(j + 1) * ROWS, pl.ds(own_col, BLK)] = (
+        before_states = x0[(j + 1) * ROWS:(j + 2) * ROWS, pl.ds(own_col, BLK)]
+        x1[(j + 1) * ROWS:(j + 2) * ROWS, pl.ds(own_col, BLK)] = (
             before_states.astype(F32) + attend(0, j)
         ).astype(BF)
         piece = x1_piece(j, x, c)
@@ -404,30 +434,33 @@
             send(piece, piece, x1_c + j, partner, None, x1_sent)
 
     def gather_states_wait(j):
-        arrive(x1.at[pl.ds(j * ROWS, ROWS), pl.ds(0, 1024)], x1_c + j)
+        arrive(x1.at[pl.ds((j + 1) * ROWS, ROWS), pl.ds(0, 1024)], x1_c + j)
 
     project(0, x0)
     ring(1, 0, 1)
     step_states(1)
+    last_send(1)
     ring(1, 1, 1)
-    arrive(kv.at[0, pl.ds(0, ROWS)], halo_f[0])
     step_states(0)
     ring(1, 0, 2)
     gather_states(1)
     ring(1, 1, 2)
+    last_spread(1)
     gather_states(0)
     ring(1, 0, 3)
     ring(1, 1, 3)
+    last_swap(1)
     gather_states_wait(1)
     gather_states_wait(0)
     ring(1, 0, 4)
     ring(1, 1, 4)
+    last_wait(1)
     project(1, x1)
 
     out_r = take("r", 2)
 
     def last_states(j):
-        before_states = x1[j * ROWS:(j + 1) * ROWS, pl.ds(own_col, BLK)]
+        before_states = x1[(j + 1) * ROWS:(j + 2) * ROWS, pl.ds(own_col, BLK)]
         x2[j * ROWS:(j + 1) * ROWS, :] = (before_states.astype(F32) + attend(1, j)).astype(BF)
         dst = outbuf.at[:, pl.ds(pl.multiple_of(xl * BLK, BLK), BLK)]
         src = x2.at[pl.ds(j * ROWS, ROWS)]
@@ -534,13 +567,12 @@
         dqkv[ROWS:, BLK:] = (dkv_last[...] + halo_recv[layer].astype(F32)).astype(BF)
         project_back(layer, 1)
 
-    last_states(1)
     for k in range(2):
         arrive(cotg.at[pl.ds(k * ROWS, ROWS)], a2a_c + k, away[k])
-    back_second(1, cotg[ROWS:, :])
-    arrive(kv.at[1, pl.ds(0, ROWS)], halo_f[1])
     last_states(0)
     back_first(1, cotg[:ROWS, :])
+    last_states(1)
+    back_second(1, cotg[ROWS:, :])
     back_own(1)
     sum_one(0)
     back_halo(1)
@@ -554,6 +586,13 @@
     sum_last(0)
     sum_last(1)
 
+    for whole, index, cond in pending:
+        copy = pltpu.make_async_remote_copy(
+            src_ref=whole, dst_ref=whole, send_sem=ssem.at[index], recv_sem=rsem.at[0],
+            device_id=partner, device_id_type=MESH,
+        )
+        when(cond, copy.wait_send)
+
     for k in range(2):
         arrive(outbuf.at[:, pl.ds(k * BLK, BLK)], out_r + k, away[k])
     out_ref[...] = outbuf[...]
@@ -565,13 +604,6 @@
         total = term if total is None else total + term
     grad_ref[...] = total
 
-    for whole, index, cond in pending:
-        copy = pltpu.make_async_remote_copy(
-            src_ref=whole, dst_ref=whole, send_sem=ssem.at[index], recv_sem=rsem.at[0],
-            device_id=partner, device_id_type=MESH,
-        )
-        when(cond, copy.wait_send)
-
     assert counts["s"] <= N_SEND and counts["r"] <= N_RECV, counts
 
 
@@ -580,8 +612,8 @@
     scratch = [
         ((2, LAYERS, 16, 3 * BLK), BF),
         ((LAYERS, 4, 8, 2, 2, 16, 3 * BLK), BF),
-        ((GROUP_ROWS, D), BF),
-        ((GROUP_ROWS, D), BF),
+        ((3 * ROWS, D), BF),
+        ((3 * ROWS, D), BF),
         ((GROUP_ROWS, BLK), BF),
         ((LAYERS, 3 * ROWS, 2 * BLK), BF),
         ((LAYERS, GROUP_ROWS, BLK), BF),

time: 107 us -> 102 us (0.953)
  Pallas kernels: 104 us -> 98.1 us
    pallas_call x1, Pallas kernels: 104 us -> 98.1 us  [per_device(): pl.pallas_call(kernel, out_shape=(jax.ShapeDtypeStruct((ROWS, 512), BF),...]
where the time goes in v4:
time: 102 us; the launch traced here: 101 us
  Pallas kernels  98.1 us (96%)
  local copies, waits for them, and re-layouts  2.32 us (2%)
    pallas_call x1, Pallas kernels, per_device(): pl.pallas_call(kernel, out_shape=(jax.ShapeDtypeStruct((ROWS, 512), BF),...  98.1 us
    unnamed x4, local copies, waits for them, and re-layouts  2.32 us

profile of v4, /device:TPU:6, one launch (start us, length us, event | category | flops | bytes accessed | tf_op | source)
XLA Modules:
  0.0 101.1 jit_solution(2947520552318541283)
XLA Ops:
  0.6 98.1 %shard_map.77 = (bf16[128,512]{1,0:T(8,128)(2,1)}, f32[128,512]{1,0:T(8,128)}) custom-call(bf16[128,512]{1,0:T(8,128)(2,1)} %x_hbm.1, bf16[128,512]{1,0:T(8,128)(2,1)} %cot_hbm.1, bf16[2,16,512]{2,1,0:T(8,128)(2,1)} %wq.1, bf16[2,16,512]{2,1,0:T(8,128)(2,1)} %wk.1, bf16[2,16,512]{2,1,0:T(8,128)(2,1)} %wv.1, s32[128]{0:T(128)} %bound_hbm.1), custom_call_target="tpu_custom_call" | custom-call | tf_op jit(solution)/shard_map/pallas_call | solution.py:636
  98.8 0.0 copy-start
  98.8 1.6 %copy.10 = bf16[128,512]{1,0:T(8,128)(2,1)} copy(bf16[128,512]{1,0:T(8,128)(2,1)} %get-tuple-element.4) | data formatting | bytes 262144
  100.4 0.0 copy-done
  100.4 0.7 copy.11
Async XLA Ops:
  98.8 1.6 %copy-start = (f32[128,512]{1,0:T(8,128)S(1)}, f32[128,512]{1,0:T(8,128)}, u32[]{:S(2)}) copy-start(f32[128,512]{1,0:T(8,128)} %get-tuple-element.5) | copy-start | bytes 786436

commit v5 on v4

--- a/solution.py
+++ b/solution.py
@@ -17,7 +17,7 @@
 SCALE = 1.0 / math.sqrt(HEAD)
 N_LOAD = 15
 N_SEND = 36
-N_RECV = 117
+N_RECV = 99
 BF = jnp.bfloat16
 F32 = jnp.float32
 
@@ -235,7 +235,7 @@
     out_z = 2 * lax.rem(z, 2) - 1
     out_y = 2 * yl - 1
     one = {(kind, rel): take("r") for kind in range(2) for rel in range(4)}
-    direct = [take("r", 7) for _ in range(2)]
+    direct = take("r", 2)
 
     def farthest(s, right):
         return 4 if (s == 0) == right else 3
@@ -243,8 +243,9 @@
     two = {
         (layer, kind, s, right, d): take("r")
         for layer in range(LAYERS) for kind in range(2) for s in range(2) for right in (False, True)
-        for d in range(1, farthest(s, right) + 1)
+        for d in range(1, 4)
     }
+    two_end = take("r", LAYERS)
 
     next_to = [
         {k: dev(x, y, wrap(z + k, 8), c) for k in (1, -1)},
@@ -287,20 +288,18 @@
         if d < farthest(s, right):
             piece = part(layer, kind, s, 0 if d == 0 else (-d if right else d))
             index = lead if right and layer + kind + s + d == 0 else batch_two[layer, kind, s]
-            send(piece, piece, two[layer, kind, s, right, d + 1], next_to[1 - kind][1 if right else -1], None, index)
+            recv = two[layer, kind, s, right, d + 1] if d < 3 else two_end + layer
+            send(piece, piece, recv, next_to[1 - kind][1 if right else -1], None, index)
 
     def ring(layer, s, d):
         for kind in range(2):
             for right in (False, True):
-                if 1 <= d <= farthest(s, right):
+                if 1 <= d <= 3:
                     arrive(part(layer, kind, s, -d if right else d), two[layer, kind, s, right, d])
-                if d <= farthest(s, right):
-                    pass_on(layer, kind, s, right, d)
-
-    def block_from(kind, k):
-        if kind == 0:
-            return w.at[0, yh, z_at[-k], yl, 0]
-        return w.at[0, y_at[-k][0], z, y_at[-k][1], 1]
+                pass_on(layer, kind, s, right, d)
+
+    def ring_end(layer):
+        arrive(w.at[layer, 0, :, :, 0], two_end + layer)
 
     def direct_send():
         for k in (1, -1, 2, -2, 3, -3, 4):
@@ -308,12 +307,11 @@
                 mine = block(0, kind, False)
                 to = wrap((z if kind == 0 else y) + k, 8)
                 target = dev(x, y, to, c) if kind == 0 else dev(x, to, z, c)
-                send(mine, mine, direct[kind] + k + 3 - (k > 0), target, None, batch_one[0][kind])
+                send(mine, mine, direct + kind, target, None, batch_one[0][kind])
 
     def direct_wait():
-        for k in (1, -1, 2, -2, 3, -3, 4):
-            for kind in range(2):
-                arrive(block_from(kind, k), direct[kind] + k + 3 - (k > 0))
+        for kind in range(2):
+            arrive(w.at[0, 0, pl.ds(0, 7), 0, kind], direct + kind)
 
     def relay(t):
         for kind in range(2):
@@ -360,8 +358,7 @@
     ring(1, 1, 0)
     last_swap(0)
     spread_cotangent()
-    ring(0, 0, 4)
-    ring(0, 1, 4)
+    ring_end(0)
     arrive(x0.at[pl.ds(0, GROUP_ROWS), pl.ds(0, 1024)], x0_c)
     last_wait(0)
 
@@ -452,8 +449,7 @@
     last_swap(1)
     gather_states_wait(1)
     gather_states_wait(0)
-    ring(1, 0, 4)
-    ring(1, 1, 4)
+    ring_end(1)
     last_wait(1)
     project(1, x1)
 
@@ -582,8 +578,8 @@
     summed_one(1)
     back_second(0, g1[ROWS:, :].astype(BF))
     back_own(0)
+    sum_last(0)
     back_halo(0)
-    sum_last(0)
     sum_last(1)
 
     for whole, index, cond in pending:

time: 102 us -> 101 us (level)
  no operation moved by 1% of the time
where the time goes in v5:
time: 101 us
  Pallas kernels  97.9 us (97%)
  local copies, waits for them, and re-layouts  2.32 us (2%)
    pallas_call x1, Pallas kernels, per_device(): pl.pallas_call(kernel, out_shape=(jax.ShapeDtypeStruct((ROWS, 512), BF),...  97.9 us
    unnamed x4, local copies, waits for them, and re-layouts  2.32 us

profile of v5, /device:TPU:6, one launch (start us, length us, event | category | flops | bytes accessed | tf_op | source)
XLA Modules:
  0.0 100.9 jit_solution(8864920862956459143)
XLA Ops:
  0.6 97.9 %shard_map.77 = (bf16[128,512]{1,0:T(8,128)(2,1)}, f32[128,512]{1,0:T(8,128)}) custom-call(bf16[128,512]{1,0:T(8,128)(2,1)} %x_hbm.1, bf16[128,512]{1,0:T(8,128)(2,1)} %cot_hbm.1, bf16[2,16,512]{2,1,0:T(8,128)(2,1)} %wq.1, bf16[2,16,512]{2,1,0:T(8,128)(2,1)} %wk.1, bf16[2,16,512]{2,1,0:T(8,128)(2,1)} %wv.1, s32[128]{0:T(128)} %bound_hbm.1), custom_call_target="tpu_custom_call" | custom-call | tf_op jit(solution)/shard_map/pallas_call | solution.py:632
  98.5 0.0 copy-start
  98.6 1.6 %copy.10 = bf16[128,512]{1,0:T(8,128)(2,1)} copy(bf16[128,512]{1,0:T(8,128)(2,1)} %get-tuple-element.4) | data formatting | bytes 262144
  100.2 0.0 copy-done
  100.2 0.7 copy.11
Async XLA Ops:
  98.5 1.6 %copy-start = (f32[128,512]{1,0:T(8,128)S(1)}, f32[128,512]{1,0:T(8,128)}, u32[]{:S(2)}) copy-start(f32[128,512]{1,0:T(8,128)} %get-tuple-element.5) | copy-start | bytes 786436

commit v6 on v5

--- a/solution.py
+++ b/solution.py
@@ -378,18 +378,18 @@
 
     halo_b = [take("r") for _ in range(LAYERS)]
 
-    def project(layer, states):
-        def columns(first, last):
+    def project(layer, states, start=0, stop=3 * ROWS):
+        def columns(row, first, last):
             total = None
             for part in range(4):
                 weight = w[layer, part].reshape(512, 3 * BLK)[:, first:last]
-                rows = slice(0 if first else ROWS, None)
-                term = nn(states[rows, part * 512:(part + 1) * 512], weight)
+                term = nn(states[row:stop, part * 512:(part + 1) * 512], weight)
                 total = term if total is None else total + term
             return total.astype(BF)
 
-        kv[layer] = columns(BLK, 3 * BLK)
-        q[layer] = columns(0, BLK)
+        kv[layer, start:stop] = columns(start, BLK, 3 * BLK)
+        own_start = max(start, ROWS)
+        q[layer, own_start - ROWS:stop - ROWS] = columns(own_start, 0, BLK)
 
     def attend(layer, j):
         visible = mask(j)
@@ -451,7 +451,7 @@
     gather_states_wait(0)
     ring_end(1)
     last_wait(1)
-    project(1, x1)
+    project(1, x1, 0, 2 * ROWS)
 
     out_r = take("r", 2)
 
@@ -567,6 +567,7 @@
         arrive(cotg.at[pl.ds(k * ROWS, ROWS)], a2a_c + k, away[k])
     last_states(0)
     back_first(1, cotg[:ROWS, :])
+    project(1, x1, 2 * ROWS, 3 * ROWS)
     last_states(1)
     back_second(1, cotg[ROWS:, :])
     back_own(1)

time: 101 us -> 101 us (level)
  no operation moved by 1% of the time
where the time goes in v6:
time: 101 us
  Pallas kernels  97.9 us (97%)
  local copies, waits for them, and re-layouts  2.32 us (2%)
    pallas_call x1, Pallas kernels, per_device(): pl.pallas_call(kernel, out_shape=(jax.ShapeDtypeStruct((ROWS, 512), BF),...  97.9 us
    unnamed x4, local copies, waits for them, and re-layouts  2.32 us

profile of v6, /device:TPU:6, one launch (start us, length us, event | category | flops | bytes accessed | tf_op | source)
XLA Modules:
  0.0 100.9 jit_solution(8724613390834955271)
XLA Ops:
  0.6 97.9 %shard_map.77 = (bf16[128,512]{1,0:T(8,128)(2,1)}, f32[128,512]{1,0:T(8,128)}) custom-call(bf16[128,512]{1,0:T(8,128)(2,1)} %x_hbm.1, bf16[128,512]{1,0:T(8,128)(2,1)} %cot_hbm.1, bf16[2,16,512]{2,1,0:T(8,128)(2,1)} %wq.1, bf16[2,16,512]{2,1,0:T(8,128)(2,1)} %wk.1, bf16[2,16,512]{2,1,0:T(8,128)(2,1)} %wv.1, s32[128]{0:T(128)} %bound_hbm.1), custom_call_target="tpu_custom_call" | custom-call | tf_op jit(solution)/shard_map/pallas_call | solution.py:633
  98.5 0.0 copy-start
  98.6 1.6 %copy.10 = bf16[128,512]{1,0:T(8,128)(2,1)} copy(bf16[128,512]{1,0:T(8,128)(2,1)} %get-tuple-element.4) | data formatting | bytes 262144
  100.2 0.0 copy-done
  100.2 0.7 copy.11
Async XLA Ops:
  98.5 1.6 %copy-start = (f32[128,512]{1,0:T(8,128)S(1)}, f32[128,512]{1,0:T(8,128)}, u32[]{:S(2)}) copy-start(f32[128,512]{1,0:T(8,128)} %get-tuple-element.5) | copy-start | bytes 786436
